TPU v7x, 32 devices: a whole 2x2x4 slice. The times are simulated.
32 devices in a mesh: batch: 4 (over y, x), strip: 8 (over z, core).
Axes of the slice: x: 2, y: 2, z: 4, core: 2. Of those that a mesh axis runs over, the one named last changes fastest.
Arguments:
- tokens: bfloat16 [4, 64, 32, 768], P('batch', 'strip'), may hold values from -6 to 6
- tile_owner: int32 [4, 4, 2], P('batch'), may hold values from 0 to 7, as said below
- time_steps: int32 [4, 8], P('batch'), may hold values from 0 to 999
- class_labels: int32 [4, 8], P('batch'), may hold values from 0 to 999
- class_embedding_matrix: bfloat16 [768, 1000], replicated, may hold values from -6 to 6
- adaptive_weight: bfloat16 [768, 4608], replicated, may hold values from -0.21875 to 0.21875
- adaptive_bias: bfloat16 [4608], replicated, may hold values from -3 to 3
- mixer_kernel: bfloat16 [768, 9], replicated, may hold values from -2 to 2
- joint_weight: bfloat16 [768, 2304], replicated, may hold values from -0.21875 to 0.21875
- output_weight: bfloat16 [768, 768], replicated, may hold values from -2.5 to 2.5
- output_bias: bfloat16 [768], replicated, may hold values from -2 to 2
- expand_weight: bfloat16 [768, 3072], replicated, may hold values from -0.21875 to 0.21875
- expand_bias: bfloat16 [3072], replicated, may hold values from -2 to 2
- hidden_kernel: bfloat16 [3072, 9], replicated, may hold values from -2 to 2
- reduce_weight: bfloat16 [3072, 768], replicated, may hold values from -0.109375 to 0.109375
- reduce_bias: bfloat16 [768], replicated, may hold values from -2 to 2
- output_cotangent: bfloat16 [4, 64, 32, 768], P('batch', 'strip'), may hold values from -6 to 6
Outputs:
- outputs: bfloat16 [4, 64, 32, 768], P('batch', 'strip')
- tokens_grad: float32 [4, 64, 32, 768], P('batch', 'strip')
- class_table_grad: float32 [768, 1000], P('strip')
- adaptive_weight_grad: float32 [768, 4608], P('strip')
- adaptive_bias_grad: float32 [4608], P('strip')
- mixer_kernel_grad: float32 [768, 9], P('strip')
- joint_weight_grad: float32 [768, 2304], P('strip')
- output_weight_grad: float32 [768, 768], P('strip')
- output_bias_grad: float32 [768], P('strip')
- expand_weight_grad: float32 [768, 3072], P('strip')
- expand_bias_grad: float32 [3072], P('strip')
- hidden_kernel_grad: float32 [3072, 9], P('strip')
- reduce_weight_grad: float32 [3072, 768], P('strip')
- reduce_bias_grad: float32 [768], P('strip')
Inputs may be any that keep to these rules, and one draw needn't show every extreme that they name: `tile_owner`: A canvas is cut into 4 x 2 tiles of 16 rows and 16 columns; the tiles of one slot form one latent, a rectangle of whole tiles; among the canvases of each index of batch, some canvas has a latent that spans all 64 rows.
All inputs are finite; a program needn't handle non-finite values.
Results may differ from a plain program's by a relative error of at most 0.023.
Values may be sent and summed in bfloat16 or wider, within the bound.
A program may use at most 320 MiB of HBM per device.

v0:
```python
import math

import jax
import jax.numpy as jnp
from jax import lax
from jax.sharding import PartitionSpec as P

HEADS = 12


EPSILON = 1e-06
MASKED = -1e30
EXACT_PRECISION = lax.Precision.HIGHEST


def padded_2(block, sides, width):
    for axis, dim in sides:
        count = lax.axis_size(axis)
        forward = [(i, i + 1) for i in range(count - 1)]
        backward = [(target, source) for source, target in forward]
        low = lax.ppermute(
            lax.slice_in_dim(block, block.shape[dim] - width, None, axis=dim), axis, forward
        )
        high = lax.ppermute(lax.slice_in_dim(block, 0, width, axis=dim), axis, backward)
        block = jnp.concatenate([low, block, high], axis=dim)
    return block


def normalize(values):
    centre = jnp.mean(values, axis=-1, keepdims=True)
    centred = values - centre
    spread = jnp.mean(centred * centred, axis=-1, keepdims=True)
    return centred * lax.rsqrt(spread + EPSILON)


def modulate(values, shifting, scaling):
    return normalize(values) * (1.0 + scaling) + shifting


def depthwise(padded, kernel):
    row_count = padded.shape[-3] - 2
    column_total = padded.shape[-2]
    widened = jnp.pad(padded, [(0, 0)] * (padded.ndim - 2) + [(1, 1), (0, 0)])
    result = jnp.zeros(
        padded.shape[:-3] + (row_count, column_total, padded.shape[-1]), padded.dtype
    )
    for tapping in range(9):
        row_shift = tapping // 3
        col_shift = tapping % 3
        window = lax.slice_in_dim(widened, row_shift, row_shift + row_count, axis=widened.ndim - 3)
        window = lax.slice_in_dim(
            window, col_shift, col_shift + column_total, axis=widened.ndim - 2
        )
        result = result + kernel[:, tapping] * window
    return result


def kernel_grad(padded, gradient):
    row_count = gradient.shape[1]
    column_total = gradient.shape[2]
    widened = jnp.pad(padded, ((0, 0), (0, 0), (1, 1), (0, 0)))
    columns = []
    for tapping in range(9):
        row_shift = tapping // 3
        col_shift = tapping % 3
        window = widened[
            :, row_shift : row_shift + row_count, col_shift : col_shift + column_total, :
        ]
        columns.append(jnp.sum(window * gradient, axis=(0, 1, 2)))
    return jnp.stack(columns, axis=1)


def timestep_features(time_steps, model_width):
    half_width = model_width // 2
    frequencies = jnp.exp(
        -math.log(10000.0) * jnp.arange(half_width, dtype=jnp.float32) / half_width
    )
    angles = time_steps.astype(jnp.float32)[..., None] * frequencies
    return jnp.concatenate([jnp.cos(angles), jnp.sin(angles)], axis=-1)


def group_owner(owner):
    canvases, row_count, column_total = owner.shape
    shaped = owner.reshape(canvases, row_count // 2, 2, column_total // 2, 2).transpose(
        0, 2, 4, 1, 3
    )
    return shaped.reshape(canvases, 2, 2, row_count // 2 * (column_total // 2))


def to_groups(tensor, head_count):
    canvases, row_count, column_total, features = tensor.shape
    head_size = features // head_count
    shaped = tensor.reshape(
        canvases, row_count // 2, 2, column_total // 2, 2, head_count, head_size
    )
    shaped = shaped.transpose(0, 2, 4, 5, 1, 3, 6)
    return shaped.reshape(
        canvases, 2, 2, head_count, row_count // 2 * (column_total // 2), head_size
    )


def from_groups(tensor, row_count, column_total):
    canvases, head_count, head_size = (tensor.shape[0], tensor.shape[3], tensor.shape[-1])
    shaped = tensor.reshape(
        canvases, 2, 2, head_count, row_count // 2, column_total // 2, head_size
    )
    shaped = shaped.transpose(0, 4, 1, 5, 2, 3, 6)
    return shaped.reshape(canvases, row_count, column_total, head_count * head_size)


def local(
    tokens,
    tile_owner,
    time_steps,
    class_labels,
    class_embedding_matrix,
    adaptive_weight,
    adaptive_bias,
    mixer_kernel,
    joint_weight,
    output_weight,
    output_bias,
    expand_weight,
    expand_bias,
    hidden_kernel,
    reduce_weight,
    reduce_bias,
    output_cotangent,
):
    canvases, row_count, column_total, model_width = tokens.shape
    head_count = HEADS
    head_size = model_width // head_count
    factor = head_size ** (-0.5)
    half_cols = column_total // 2
    strips = lax.axis_size("strip")
    strip_index = lax.axis_index("strip")
    canvas_rows = row_count * strips
    class_count = class_embedding_matrix.shape[1]
    latent_count = time_steps.shape[1]
    tile_rows = canvas_rows // 4
    full_owner = jnp.broadcast_to(
        tile_owner[:, :, None, :, None], (canvases, 4, tile_rows, 2, half_cols)
    ).reshape(canvases, canvas_rows, column_total)
    local_owner = lax.dynamic_slice_in_dim(full_owner, strip_index * row_count, row_count, 1)
    token_hot = (local_owner[..., None] == jnp.arange(latent_count, dtype=jnp.int32)).astype(
        jnp.float32
    )
    class_onehot = (class_labels[..., None] == jnp.arange(class_count, dtype=jnp.int32)).astype(
        jnp.bfloat16
    )
    class_rows = jnp.einsum(
        "ywj,gj->ywg", class_onehot, class_embedding_matrix, preferred_element_type=jnp.float32
    )
    condition = timestep_features(time_steps, model_width) + class_rows
    silu_value, silu_pull = jax.vjp(jax.nn.silu, condition)
    silu_cond = silu_value.astype(jnp.bfloat16)
    modulation = jnp.einsum(
        "cbd,de->cbe", silu_cond, adaptive_weight, preferred_element_type=jnp.float32
    )
    modulation = modulation + adaptive_bias.astype(jnp.float32)
    token_mod = jnp.einsum("crkb,cbe->crke", token_hot, modulation, precision=EXACT_PRECISION)
    shift_one, scale_one, gate_one, shift_two, scale_two, gate_two = jnp.split(
        token_mod, 6, axis=-1
    )
    inputs = tokens.astype(jnp.float32)
    first_value, first_pull = jax.vjp(modulate, inputs, shift_one, scale_one)
    first = first_value.astype(jnp.bfloat16)
    first_padded = padded_2(first, (("strip", 1),), 1)
    mixer_single_float = mixer_kernel.astype(jnp.float32)
    mixed = depthwise(first_padded.astype(jnp.float32), mixer_single_float).astype(jnp.bfloat16)
    joint = jnp.einsum("crkd,de->crke", mixed, joint_weight, preferred_element_type=jnp.float32)
    query_rows = joint[..., :model_width].astype(jnp.bfloat16)
    keys_local = joint[..., model_width : 2 * model_width].astype(jnp.bfloat16)
    values_local = joint[..., 2 * model_width :].astype(jnp.bfloat16)
    keys_canvas, values_canvas = (
        lax.all_gather(keys_local, "strip", axis=1, tiled=True),
        lax.all_gather(values_local, "strip", axis=1, tiled=True),
    )
    query_groups = to_groups(query_rows, head_count)
    key_groups = to_groups(keys_canvas, head_count)
    value_groups = to_groups(values_canvas, head_count)
    query_owner = group_owner(local_owner)
    key_owner = group_owner(full_owner)
    allowed = (query_owner[..., :, None] == key_owner[..., None, :])[:, :, :, None]

    def attention_scores():
        raw = (
            jnp.einsum(
                "cabhnd,cabhmd->cabhnm",
                query_groups,
                key_groups,
                preferred_element_type=jnp.float32,
            )
            * factor
        )
        return jnp.where(allowed, raw, MASKED)

    scores = attention_scores()
    peak = jnp.max(scores, axis=-1, keepdims=True)
    lifted_float = jnp.exp(scores - peak)
    total = jnp.sum(lifted_float, axis=-1, keepdims=True)
    softened = (lifted_float / total).astype(jnp.bfloat16)
    log_total = peak + jnp.log(total)
    attended_groups = jnp.einsum(
        "cabhnm,cabhmd->cabhnd", softened, value_groups, preferred_element_type=jnp.float32
    )
    attended = from_groups(attended_groups, row_count, column_total).astype(jnp.bfloat16)
    branch_one = jnp.einsum(
        "crkd,de->crke", attended, output_weight, preferred_element_type=jnp.float32
    )
    branch_one = branch_one + output_bias.astype(jnp.float32)
    residual = inputs + gate_one * branch_one
    second_value, second_pull = jax.vjp(modulate, residual, shift_two, scale_two)
    second = second_value.astype(jnp.bfloat16)
    expanded = jnp.einsum(
        "crkd,df->crkf", second, expand_weight, preferred_element_type=jnp.float32
    )
    expanded = (expanded + expand_bias.astype(jnp.float32)).astype(jnp.bfloat16)
    expanded_padded = padded_2(expanded, (("strip", 1),), 1)
    hidden_float = hidden_kernel.astype(jnp.float32)
    conv_out = depthwise(expanded_padded.astype(jnp.float32), hidden_float)
    gelu_value, gelu_pull = jax.vjp(jax.nn.gelu, conv_out)
    activated = gelu_value.astype(jnp.bfloat16)
    branch_two = jnp.einsum(
        "crkf,fd->crkd", activated, reduce_weight, preferred_element_type=jnp.float32
    )
    branch_two = branch_two + reduce_bias.astype(jnp.float32)
    outputs = (residual + gate_two * branch_two).astype(jnp.bfloat16)
    upstream = output_cotangent.astype(jnp.float32)
    two_grad = (upstream * gate_two).astype(jnp.bfloat16)
    gate_two_grad = upstream * branch_two
    reduce_bias_grad = jnp.sum(two_grad.astype(jnp.float32), axis=(0, 1, 2))
    reduce_weight_grad = jnp.einsum(
        "crkf,crkd->fd", activated, two_grad, preferred_element_type=jnp.float32
    )
    activated_grad = jnp.einsum(
        "crkd,fd->crkf", two_grad, reduce_weight, preferred_element_type=jnp.float32
    )
    conv_grad = gelu_pull(activated_grad)[0].astype(jnp.bfloat16)
    conv_padded = padded_2(conv_grad, (("strip", 1),), 1)
    expanded_grad = depthwise(conv_padded.astype(jnp.float32), hidden_float[:, ::-1]).astype(
        jnp.bfloat16
    )
    hidden_kernel_grad = kernel_grad(
        expanded_padded.astype(jnp.float32), conv_grad.astype(jnp.float32)
    )
    expand_bias_grad = jnp.sum(expanded_grad.astype(jnp.float32), axis=(0, 1, 2))
    expand_weight_grad = jnp.einsum(
        "crkd,crkf->df", second, expanded_grad, preferred_element_type=jnp.float32
    )
    second_grad = jnp.einsum(
        "crkf,df->crkd", expanded_grad, expand_weight, preferred_element_type=jnp.float32
    )
    residual_part, shift_two_grad, scale_two_grad = second_pull(second_grad)
    residual_grad = upstream + residual_part
    gate_one_grad = residual_grad * branch_one
    one_grad = (residual_grad * gate_one).astype(jnp.bfloat16)
    output_bias_grad = jnp.sum(one_grad.astype(jnp.float32), axis=(0, 1, 2))
    output_weight_grad = jnp.einsum(
        "crkd,crke->de", attended, one_grad, preferred_element_type=jnp.float32
    )
    attended_grad = jnp.einsum(
        "crke,de->crkd", one_grad, output_weight, preferred_element_type=jnp.float32
    ).astype(jnp.bfloat16)
    attended_grad_groups = to_groups(attended_grad, head_count)
    probs = jnp.exp(attention_scores() - log_total)
    prob_grads = jnp.einsum(
        "cabhnd,cabhmd->cabhnm",
        attended_grad_groups,
        value_groups,
        preferred_element_type=jnp.float32,
    )
    spread_sum = jnp.sum(probs * prob_grads, axis=-1, keepdims=True)
    score_grads = (probs * (prob_grads - spread_sum)).astype(jnp.bfloat16)
    query_grad_groups = (
        jnp.einsum(
            "cabhnm,cabhmd->cabhnd", score_grads, key_groups, preferred_element_type=jnp.float32
        )
        * factor
    )
    query_grad = from_groups(query_grad_groups, row_count, column_total).astype(jnp.bfloat16)
    all_queries, all_attended = (
        lax.all_gather(query_groups, "strip", axis=4, tiled=True),
        lax.all_gather(attended_grad_groups, "strip", axis=4, tiled=True),
    )
    all_logs, all_spreads = (
        lax.all_gather(log_total[..., 0], "strip", axis=4, tiled=True),
        lax.all_gather(spread_sum[..., 0], "strip", axis=4, tiled=True),
    )
    own_keys = to_groups(keys_local, head_count)
    own_values = to_groups(values_local, head_count)
    own_allowed = (key_owner[..., :, None] == query_owner[..., None, :])[:, :, :, None]
    own_scores = (
        jnp.einsum(
            "cabhnd,cabhmd->cabhnm", all_queries, own_keys, preferred_element_type=jnp.float32
        )
        * factor
    )
    own_scores = jnp.where(own_allowed, own_scores, MASKED)
    own_probs = jnp.exp(own_scores - all_logs[..., None])
    own_prob_grads = jnp.einsum(
        "cabhnd,cabhmd->cabhnm", all_attended, own_values, preferred_element_type=jnp.float32
    )
    own_score_grads = (own_probs * (own_prob_grads - all_spreads[..., None])).astype(jnp.bfloat16)
    key_grad_groups = (
        jnp.einsum(
            "cabhnm,cabhnd->cabhmd",
            own_score_grads,
            all_queries,
            preferred_element_type=jnp.float32,
        )
        * factor
    )
    value_grad_groups = jnp.einsum(
        "cabhnm,cabhnd->cabhmd",
        own_probs.astype(jnp.bfloat16),
        all_attended,
        preferred_element_type=jnp.float32,
    )
    key_grad = from_groups(key_grad_groups, row_count, column_total).astype(jnp.bfloat16)
    value_grad = from_groups(value_grad_groups, row_count, column_total).astype(jnp.bfloat16)
    joint_grad = jnp.concatenate([query_grad, key_grad, value_grad], axis=-1)
    joint_weight_grad = jnp.einsum(
        "crkd,crke->de", mixed, joint_grad, preferred_element_type=jnp.float32
    )
    mixed_grad = jnp.einsum(
        "crke,de->crkd", joint_grad, joint_weight, preferred_element_type=jnp.float32
    ).astype(jnp.bfloat16)
    mixed_padded = padded_2(mixed_grad, (("strip", 1),), 1)
    first_grad = depthwise(mixed_padded.astype(jnp.float32), mixer_single_float[:, ::-1])
    mixer_kernel_grad = kernel_grad(
        first_padded.astype(jnp.float32), mixed_grad.astype(jnp.float32)
    )
    input_part, shift_one_grad, scale_one_grad = first_pull(first_grad)
    tokens_grad = residual_grad + input_part
    token_grad = jnp.concatenate(
        [
            shift_one_grad,
            scale_one_grad,
            gate_one_grad,
            shift_two_grad,
            scale_two_grad,
            gate_two_grad,
        ],
        axis=-1,
    )
    modulation_grad = jnp.einsum("crkb,crke->cbe", token_hot, token_grad, precision=EXACT_PRECISION)
    silu_grad = jnp.einsum(
        "cbe,de->cbd",
        modulation_grad,
        adaptive_weight.astype(jnp.float32),
        precision=EXACT_PRECISION,
    )
    conditioning_grad = silu_pull(silu_grad)[0]
    table_grad = jnp.einsum(
        "soy,sok->yk",
        conditioning_grad,
        class_onehot.astype(jnp.float32),
        precision=EXACT_PRECISION,
    )
    adaptive_grad = jnp.einsum(
        "cbd,cbe->de", silu_cond.astype(jnp.float32), modulation_grad, precision=EXACT_PRECISION
    )
    adaptive_bias_grad = jnp.sum(modulation_grad, axis=(0, 1))
    (
        table_shard,
        adaptive_shard,
        adaptive_bias_shard,
        mixer_shard,
        joint_shard,
        output_shard,
        output_bias_shard,
        expand_shard,
        expand_bias_shard,
        hidden_shard,
        reduce_shard,
        reduce_bias_shard,
    ) = (
        lax.psum_scatter(
            table_grad.astype(jnp.bfloat16), "strip", scatter_dimension=0, tiled=True
        ).astype(jnp.float32),
        lax.psum_scatter(
            adaptive_grad.astype(jnp.bfloat16), "strip", scatter_dimension=0, tiled=True
        ).astype(jnp.float32),
        lax.psum_scatter(
            adaptive_bias_grad.astype(jnp.bfloat16), "strip", scatter_dimension=0, tiled=True
        ).astype(jnp.float32),
        lax.psum_scatter(
            mixer_kernel_grad.astype(jnp.bfloat16), "strip", scatter_dimension=0, tiled=True
        ).astype(jnp.float32),
        lax.psum_scatter(
            joint_weight_grad.astype(jnp.bfloat16), "strip", scatter_dimension=0, tiled=True
        ).astype(jnp.float32),
        lax.psum_scatter(
            output_weight_grad.astype(jnp.bfloat16), "strip", scatter_dimension=0, tiled=True
        ).astype(jnp.float32),
        lax.psum_scatter(
            output_bias_grad.astype(jnp.bfloat16), "strip", scatter_dimension=0, tiled=True
        ).astype(jnp.float32),
        lax.psum_scatter(
            expand_weight_grad.astype(jnp.bfloat16), "strip", scatter_dimension=0, tiled=True
        ).astype(jnp.float32),
        lax.psum_scatter(
            expand_bias_grad.astype(jnp.bfloat16), "strip", scatter_dimension=0, tiled=True
        ).astype(jnp.float32),
        lax.psum_scatter(
            hidden_kernel_grad.astype(jnp.bfloat16), "strip", scatter_dimension=0, tiled=True
        ).astype(jnp.float32),
        lax.psum_scatter(
            reduce_weight_grad.astype(jnp.bfloat16), "strip", scatter_dimension=0, tiled=True
        ).astype(jnp.float32),
        lax.psum_scatter(
            reduce_bias_grad.astype(jnp.bfloat16), "strip", scatter_dimension=0, tiled=True
        ).astype(jnp.float32),
    )
    summed = (
        lax.psum(table_shard.astype(jnp.bfloat16), "batch").astype(jnp.float32),
        lax.psum(adaptive_shard.astype(jnp.bfloat16), "batch").astype(jnp.float32),
        lax.psum(adaptive_bias_shard.astype(jnp.bfloat16), "batch").astype(jnp.float32),
        lax.psum(mixer_shard.astype(jnp.bfloat16), "batch").astype(jnp.float32),
        lax.psum(joint_shard.astype(jnp.bfloat16), "batch").astype(jnp.float32),
        lax.psum(output_shard.astype(jnp.bfloat16), "batch").astype(jnp.float32),
        lax.psum(output_bias_shard.astype(jnp.bfloat16), "batch").astype(jnp.float32),
        lax.psum(expand_shard.astype(jnp.bfloat16), "batch").astype(jnp.float32),
        lax.psum(expand_bias_shard.astype(jnp.bfloat16), "batch").astype(jnp.float32),
        lax.psum(hidden_shard.astype(jnp.bfloat16), "batch").astype(jnp.float32),
        lax.psum(reduce_shard.astype(jnp.bfloat16), "batch").astype(jnp.float32),
        lax.psum(reduce_bias_shard.astype(jnp.bfloat16), "batch").astype(jnp.float32),
    )
    return (
        outputs,
        tokens_grad,
        summed[0],
        summed[1],
        summed[2],
        summed[3],
        summed[4],
        summed[5],
        summed[6],
        summed[7],
        summed[8],
        summed[9],
        summed[10],
        summed[11],
    )


def solution(mesh):
    return jax.shard_map(
        local,
        mesh=mesh,
        in_specs=(
            P("batch", "strip", None, None),
            P("batch", None, None),
            P("batch", None),
            P("batch", None),
            P(),
            P(),
            P(),
            P(),
            P(),
            P(),
            P(),
            P(),
            P(),
            P(),
            P(),
            P(),
            P("batch", "strip", None, None),
        ),
        out_specs=(
            P("batch", "strip", None, None),
            P("batch", "strip", None, None),
            P("strip", None),
            P("strip", None),
            P("strip"),
            P("strip", None),
            P("strip", None),
            P("strip", None),
            P("strip"),
            P("strip", None),
            P("strip"),
            P("strip", None),
            P("strip", None),
            P("strip"),
        ),
        check_vma=False,
    )
```

profile of v0, /device:TPU:0, one launch (start us, length us, event | category | flops | bytes accessed | tf_op | source)
XLA Modules:
  0.0 871.0 jit_solution(17400813760858239700)
XLA Ops:
  54.8 25.3 %all-gather.7.cloned.1.call-done = bf16[1,64,32,768]{3,2,0,1:T(8,128)(2,1)} async-done(((bf16[1,8,32,768]{3,2,0,1:T(8,128)(2,1)}), bf16[1,64,32,768]{3,2,0,1:T(8,128)(2,1)}) %all-gather.7.cloned.1.call-update) | async-done | bytes 3145744 | tf_op jit(solution)/shard_map/all_gather | solution.py:176
  80.2 10.6 %reshape.845 = bf16[1,32,2,16,2,12,64]{6,5,4,3,2,1,0:T(8,128)(2,1)} reshape(bf16[1,64,32,768]{3,2,0,1:T(8,128)(2,1)} %all-gather.7.cloned.1.call-done) | data formatting | bytes 6291456 | tf_op jit(solution)/shard_map/reshape | solution.py:93
  90.8 8.5 copy.124
  99.3 20.2 %all-gather.9.cloned.1.call-done = bf16[1,64,32,768]{3,2,0,1:T(8,128)(2,1)} async-done(((bf16[1,8,32,768]{3,2,0,1:T(8,128)(2,1)}), bf16[1,64,32,768]{3,2,0,1:T(8,128)(2,1)}) %all-gather.9.cloned.1.call-update) | async-done | bytes 3145744 | tf_op jit(solution)/shard_map/all_gather | solution.py:177
  119.5 10.6 %reshape.847 = bf16[1,32,2,16,2,12,64]{6,5,4,3,2,1,0:T(8,128)(2,1)} reshape(bf16[1,64,32,768]{3,2,0,1:T(8,128)(2,1)} %all-gather.9.cloned.1.call-done) | data formatting | bytes 6291456 | tf_op jit(solution)/shard_map/reshape | solution.py:93
  130.2 8.6 copy.127
  177.9 18.6 %fusion.63 = (bf16[3072]{0:T(1024)(128)(2,1)}, bf16[3072]{0:T(1024)(128)(2,1)}, bf16[3072]{0:T(1024)(128)(2,1)}, bf16[3072]{0:T(1024)(128)(2,1)}, bf16[3072]{0:T...) fusion(f32[1,10,32,3072]{3,2,1,0:T(8,128)} %copy-done.2, ...), kind=kOutput, calls=%fused_computation.93 | convolution fusion | flops 1238602752 | bytes 23255040 | tf_op jit(solution)/shard_map/crkd,fd->crkf/dot_general | solution.py:236
  245.1 36.2 %all-gather = f32[2,2,12,512]{2,1,0,3:T(2,128)} all-gather(f32[2,2,12,64]{2,1,0,3:T(2,128)} %copy.138), channel_id=2, replica_groups=mesh['batch'=4,'strip'=8] {'strip'}, dimensions={3}, use_global_device_ids=true | all-gather | bytes 110592 | tf_op jit(solution)/shard_map/all_gather | solution.py:287
  283.5 15.4 %copy.136 = bf16[1,2,2,12,512,64]{4,5,3,2,1,0:T(8,128)(2,1)} copy(bf16[1,2,2,12,512,64]{5,2,3,1,0,4:T(2,128)(2,1)} %all-gather.11.cloned.1.call-done) | data formatting | bytes 6291456 | tf_op jit(solution)/shard_map/all_gather | solution.py:283
  304.8 10.7 %multiply_reduce_fusion = (f32[2,2,12,64]{3,2,1,0:T(8,128)}, f32[2,2,12,64,512]{4,3,2,1,0:T(8,128)}) fusion(f32[2,2,12,64,512]{4,3,2,1,0:T(8,128)} %copy-done.1, f32[2,2,12,64]{3,2,1,0:T(8,128)S(1)} %copy-done.36, pred[2,2,64,512]{3,2,1,0:T(8,128)(4,1)S(1)} %copy-done.22, bf16[2,2,12,64,64]{4,3,2,1,0:T(8,128)(2,1)S(1)} %bitcast.248, ...), kind=kOutput, calls=%fused_computation.17 | convolution fusion | flops 209187840 | bytes 16277504 | tf_op jit(solution)/shard_map/cabhnd,cabhmd->cabhnm/dot_general | solution.py:267
  316.9 8.0 multiply_convert_fusion.6
  329.0 18.1 %all-gather.1 = f32[2,2,12,512]{2,1,0,3:T(2,128)} all-gather(f32[2,2,12,64]{2,1,0,3:T(2,128)} %copy.144), channel_id=3, replica_groups=mesh['batch'=4,'strip'=8] {'strip'}, dimensions={3}, use_global_device_ids=true | all-gather | bytes 110592 | tf_op jit(solution)/shard_map/all_gather | solution.py:288
  349.4 15.3 %copy.142 = bf16[1,2,2,12,512,64]{4,5,3,2,1,0:T(8,128)(2,1)} copy(bf16[1,2,2,12,512,64]{5,2,3,1,0,4:T(2,128)(2,1)} %all-gather.13.cloned.1.call-done) | data formatting | bytes 6291456 | tf_op jit(solution)/shard_map/all_gather | solution.py:284
  370.8 8.4 multiply_convert_fusion.5
  440.9 8.7 %convolution_convert_fusion = bf16[768,4608]{1,0:T(8,128)(2,1)} fusion(f32[8,4608]{1,0:T(8,128)} %copy-done.32, f32[8,768]{1,0:T(8,128)} %copy-done.37), kind=kOutput, calls=%fused_computation.11 | convolution fusion | flops 343308288 | bytes 7249920 | tf_op jit(solution)/shard_map/cbd,cbe->de/dot_general | solution.py:361
  478.4 48.2 %reduce-scatter.23.cloned.1.call-done = bf16[384,768]{1,0:T(8,128)(2,1)} async-done(((bf16[3072,768]{1,0:T(8,128)(2,1)}), bf16[384,768]{1,0:T(8,128)(2,1)}) %reduce-scatter.23.cloned.1.call-update) | async-done | bytes 589840 | tf_op jit(solution)/shard_map/reduce_scatter | solution.py:409
  526.6 55.7 %reduce-scatter.21.cloned.1.call-done = bf16[96,3072]{1,0:T(8,128)(2,1)} async-done(((bf16[768,3072]{1,0:T(8,128)(2,1)}), bf16[96,3072]{1,0:T(8,128)(2,1)}) %reduce-scatter.21.cloned.1.call-update) | async-done | bytes 589840 | tf_op jit(solution)/shard_map/reduce_scatter | solution.py:400
  582.2 44.5 %reduce-scatter.17.cloned.1.call-done = bf16[96,2304]{1,0:T(8,128)(2,1)} async-done(((bf16[768,2304]{1,0:T(8,128)(2,1)}), bf16[96,2304]{1,0:T(8,128)(2,1)}) %reduce-scatter.17.cloned.1.call-update) | async-done | bytes 442384 | tf_op jit(solution)/shard_map/reduce_scatter | solution.py:391
  626.8 78.1 %reduce-scatter.15.cloned.1.call-done = bf16[96,4608]{1,0:T(8,128)(2,1)} async-done(((bf16[768,4608]{1,0:T(8,128)(2,1)}), bf16[96,4608]{1,0:T(8,128)(2,1)}) %reduce-scatter.15.cloned.1.call-update) | async-done | bytes 884752 | tf_op jit(solution)/shard_map/reduce_scatter | solution.py:382
  708.0 29.7 %reduce-scatter.27.cloned.1.call-done = bf16[384,9]{1,0:T(8,128)(2,1)} async-done(((bf16[3072,9]{1,0:T(8,128)(2,1)}), bf16[384,9]{1,0:T(8,128)(2,1)}) %reduce-scatter.27.cloned.1.call-update) | async-done | bytes 6928
  738.7 30.3 %reduce-scatter.25.cloned.1.call-done = bf16[96,9]{1,0:T(8,128)(2,1)} async-done(((bf16[768,9]{1,0:T(8,128)(2,1)}), bf16[96,9]{1,0:T(8,128)(2,1)}) %reduce-scatter.25.cloned.1.call-update) | async-done | bytes 1744
  769.8 27.2 %all-reduce.8 = (bf16[4608]{0:T(1024)(128)(2,1)}, bf16[768]{0:T(1024)(128)(2,1)}, bf16[3072]{0:T(1024)(128)(2,1)}, bf16[768]{0:T(1024)(128)(2,1)}) all-reduce(bf16[4608]{0:T(1024)(128)(2,1)} %get-tuple-element.104, bf16[768]{0:T(1024)(128)(2,1)} %get-tuple-element.61, ...), channel_id=6, replica_groups=mesh['batch'=4,'strip'=8] {'strip'}, use_global_device_ids=true, to_apply=%region_16.17.clone | all-reduce | flops 9216 | bytes 36864
  802.1 18.0 %all-reduce.9 = (bf16[576]{0:T(1024)(128)(2,1)}, bf16[96,9]{0,1:T(8,128)(2,1)}, bf16[96]{0:T(256)(128)(2,1)}, bf16[384]{0:T(512)(128)(2,1)}, bf16[384,9]{0,1:T(8,128)(2,1)}, /*index=5*/bf16[96]{0:T(256)(128)(2,1)}) all-reduce(bf16[576]{0:T(1024)(128)(2,1)} %dynamic-slice.2, ...), channel_id=1, replica_groups=mesh['batch'=4,'strip'=8] {'batch'}, use_global_device_ids=true, to_apply=%region_17.18 | all-reduce | flops 5472 | bytes 21888 | tf_op jit(solution)/shard_map/psum | solution.py:419
  827.6 27.9 %all-reduce.13.cloned.1.call-done = (bf16[96,1000]{1,0:T(8,128)(2,1)}, bf16[96,4608]{1,0:T(8,128)(2,1)}, bf16[96,2304]{1,0:T(8,128)(2,1)}, bf16[96,768]{1,0:T(8,...) async-done(((bf16[96,1000]{1,0:T(8,128)(2,1)}, bf16[96,4608]{1,0:T(8,128)(2,1)}, bf16[96,2304]{1,0:T(8,128)(2,1)}, bf16[96,768]{1,0:T(8,128)(2,1)}, ...) | async-done | bytes 2846224 | tf_op jit(solution)/shard_map/psum | solution.py:417
  (386 shorter events, 270.6 us)
Async XLA Ops:
  7.2 29.2 %copy-start = (bf16[768,2304]{1,0:T(8,128)(2,1)S(1)}, bf16[768,2304]{1,0:T(8,128)(2,1)}, u32[]{:S(2)}) copy-start(bf16[768,2304]{1,0:T(8,128)(2,1)} %param.25) | copy-start | bytes 10616836
  7.2 73.0 %all-gather.7.cloned.1.call-start = ((), (), s32[]{:S(2)}) async-start(), calls=%async_computation.8 | async-start | bytes 3538944 | tf_op jit(solution)/shard_map/all_gather | solution.py:176
  11.9 27.9 %copy-start.65 = (s32[8,32]{1,0:T(8,128)}, s32[8,32]{1,0:T(8,128)S(1)}, u32[]{:S(2)}) copy-start(s32[8,32]{1,0:T(8,128)S(1)} %copy.118) | copy-start | bytes 3076
  28.0 3.9 collective-permute-start
  30.4 5.3 collective-permute-start.1
  39.0 80.5 %all-gather.9.cloned.1.call-start = ((), (), s32[]{:S(2)}) async-start(), calls=%async_computation.9 | async-start | bytes 3538944 | tf_op jit(solution)/shard_map/all_gather | solution.py:177
  39.8 243.8 %all-gather.11.cloned.1.call-start = ((), (), s32[]{:S(2)}) async-start(), calls=%async_computation.10 | async-start | bytes 7077888 | tf_op jit(solution)/shard_map/all_gather | solution.py:283
  164.1 8.6 collective-permute-start.2
  166.9 5.7 collective-permute-start.3
  172.6 176.8 %all-gather.13.cloned.1.call-start = ((), (), s32[]{:S(2)}) async-start(), calls=%async_computation.11 | async-start | bytes 7077888 | tf_op jit(solution)/shard_map/all_gather | solution.py:284
  177.9 37.8 %copy-start.23 = (f32[1,8,32,3072]{3,2,1,0:T(8,128)}, f32[1,8,32,3072]{3,2,1,0:T(8,128)S(1)}, u32[]{:S(2)}) copy-start(f32[1,8,32,3072]{3,2,1,0:T(8,128)S(1)} %multiply_add_fusion) | copy-start | bytes 9437188
  197.6 5.3 collective-permute-start.4
  200.9 3.7 collective-permute-start.5
  230.9 247.4 %reduce-scatter.19.cloned.1.call-start = ((), (), s32[]{:S(2)}) async-start(), calls=%async_computation.15 | async-start | bytes 1327104 | tf_op jit(solution)/shard_map/reduce_scatter | solution.py:394
  397.7 6.2 collective-permute-start.6
  400.6 3.6 collective-permute-start.7
  403.6 74.8 %reduce-scatter.13.cloned.1.call-start = ((), (), s32[]{:S(2)}) async-start(), calls=%async_computation.12 | async-start | bytes 1769472 | tf_op jit(solution)/shard_map/reduce_scatter | solution.py:379
  424.6 102.0 %reduce-scatter.23.cloned.1.call-start = ((), (), s32[]{:S(2)}) async-start(), calls=%async_computation.17 | async-start | bytes 5308416 | tf_op jit(solution)/shard_map/reduce_scatter | solution.py:409
  431.1 151.1 %reduce-scatter.21.cloned.1.call-start = ((), (), s32[]{:S(2)}) async-start(), calls=%async_computation.16 | async-start | bytes 5308416 | tf_op jit(solution)/shard_map/reduce_scatter | solution.py:400
  436.3 190.5 %reduce-scatter.17.cloned.1.call-start = ((), (), s32[]{:S(2)}) async-start(), calls=%async_computation.14 | async-start | bytes 3981312 | tf_op jit(solution)/shard_map/reduce_scatter | solution.py:391
  440.6 264.2 %reduce-scatter.15.cloned.1.call-start = ((), (), s32[]{:S(2)}) async-start(), calls=%async_computation.13 | async-start | bytes 7962624 | tf_op jit(solution)/shard_map/reduce_scatter | solution.py:382
  449.7 288.0 %reduce-scatter.27.cloned.1.call-start = ((), (), s32[]{:S(2)}) async-start(), calls=%async_computation.19 | async-start | bytes 884736
  465.8 303.1 %reduce-scatter.25.cloned.1.call-start = ((), (), s32[]{:S(2)}) async-start(), calls=%async_computation.18 | async-start | bytes 221184
  478.3 377.2 %all-reduce.13.cloned.1.call-start = ((), (), s32[]{:S(2)}) async-start(), calls=%async_computation.20 | async-start | bytes 5701632 | tf_op jit(solution)/shard_map/psum | solution.py:417
  (94 other events, 460.2 us)
Sparse Core Ops, SparseCore 0:
  39.1 41.0 all-gather.6
  82.4 37.1 all-gather.8
  172.7 67.0 all-gather.10
  241.9 73.2 all-gather.12
  403.7 32.3 reduce-scatter.18
  438.8 32.4 reduce-scatter.12
  473.7 52.8 reduce-scatter.22
  528.9 53.3 reduce-scatter.20
  584.6 42.1 reduce-scatter.16
  629.0 75.7 reduce-scatter.14
  707.8 29.8 reduce-scatter.26
  740.4 28.5 reduce-scatter.24
  773.3 82.1 all-reduce.12
where the time goes:
time: 880 us; the launch traced here: 871 us
  waiting for transfers between devices  367 us (42%)
  local copies, waits for them, and re-layouts  180 us (20%)
  matrix products  133 us (15%)
  blocking collectives  99.5 us (11%)
  other arithmetic  56 us (6%)
  starting transfers between devices  17.7 us (2%)
  between operations  17.7 us (2%)
    reduce_scatter x1, waiting for transfers between devices, local(): lax.psum_scatter(adaptive_grad.astype(jnp.bfloat16), 'strip', scatter_dim...  78.1 us
    unnamed x15, waiting for transfers between devices  60.8 us
    reduce_scatter x1, waiting for transfers between devices, local(): lax.psum_scatter(expand_weight_grad.astype(jnp.bfloat16), 'strip', scatte...  55.7 us
    reduce_scatter x1, waiting for transfers between devices, local(): lax.psum_scatter(reduce_weight_grad.astype(jnp.bfloat16), 'strip', scatte...  48.2 us
    reduce_scatter x1, waiting for transfers between devices, local(): lax.psum_scatter(joint_weight_grad.astype(jnp.bfloat16), 'strip', scatter...  44.5 us
    all_gather x1, blocking collectives, local(): lax.all_gather(log_total[..., 0], 'strip', axis=4, tiled=True)  36.2 us
    reshape x6, local copies, waits for them, and re-layouts, to_groups(): tensor.reshape(canvases, row_count // 2, 2, column_total // 2, 2, head_co...  31.1 us
    psum x1, waiting for transfers between devices, local(): lax.psum(table_shard.astype(jnp.bfloat16), 'batch').astype(jnp.float32)  27.9 us
  transfers between devices with their start and end apart: 21, of which 12 were waited for; matrix products, arithmetic and copies ran while one was open for 28% of the time, Pallas kernels for 0%

commit v1 on v0

--- a/solution.py
+++ b/solution.py
@@ -1,15 +1,1469 @@
+import functools
 import math
 
 import jax
 import jax.numpy as jnp
 from jax import lax
+from jax.experimental import pallas as pl
+from jax.experimental.pallas import tpu as pltpu
 from jax.sharding import PartitionSpec as P
 
 HEADS = 12
-
-
 EPSILON = 1e-06
 MASKED = -1e30
+MESH = pl.DeviceIdType.MESH
+F32 = jnp.float32
+BF16 = jnp.bfloat16
+VMEM_BYTES = 56 * 1024 * 1024
+WHOLE = pl.BlockSpec(memory_space=pltpu.VMEM)
+LEFT = pl.BlockSpec(memory_space=pl.ANY)
+SCALARS = pl.BlockSpec(memory_space=pltpu.SMEM)
+NT = (((1,), (1,)), ((), ()))
+TN = (((0,), (0,)), ((), ()))
+
+
+def rcopy(src, dst, send, recv, strip):
+    return pltpu.make_async_remote_copy(
+        src_ref=src,
+        dst_ref=dst,
+        send_sem=send,
+        recv_sem=recv,
+        device_id=(lax.axis_index("batch"), strip),
+        device_id_type=MESH,
+    )
+
+
+def strip_barrier(strips):
+    me = lax.axis_index("strip")
+    barrier = pltpu.get_barrier_semaphore()
+    for d in range(1, strips):
+        pl.semaphore_signal(
+            barrier,
+            inc=1,
+            device_id=(lax.axis_index("batch"), lax.rem(me + d, strips)),
+            device_id_type=MESH,
+        )
+    pl.semaphore_wait(barrier, strips - 1)
+
+
+def spread(mod, width):
+    return jnp.concatenate(
+        [jnp.broadcast_to(mod[0:1], (8, width)), jnp.broadcast_to(mod[1:2], (8, width))], axis=0
+    )
+
+
+def spread_columns(buffer, r, x):
+    for k in range(x.shape[-1] // 128):
+        buffer[r, k] = x[:, k * 128 : k * 128 + 128]
+
+
+def every_second(buffer, r, p):
+    return jnp.concatenate(
+        [buffer[r, k, pl.ds(p, 16, stride=2), :] for k in range(buffer.shape[1])], axis=-1
+    )
+
+
+def ln_parts(x):
+    centre = jnp.mean(x, axis=-1, keepdims=True)
+    centred = x - centre
+    var = jnp.mean(centred * centred, axis=-1, keepdims=True)
+    inv = lax.rsqrt(var + EPSILON)
+    return centred * inv, inv
+
+
+def shifts(even, odd):
+    j = lax.broadcasted_iota(jnp.int32, even.shape, 0)
+    n = even.shape[0]
+    odd_m = jnp.where(j == 0, 0.0, pltpu.roll(odd, 1, 0))
+    even_p = jnp.where(j == n - 1, 0.0, pltpu.roll(even, n - 1, 0))
+    return odd_m, even_p
+
+
+def conv_row(load, weights, flip):
+    out0 = out1 = None
+    for i in range(3):
+        even, odd = load(i)
+        odd_m, even_p = shifts(even, odd)
+        t = [weights[8 - (3 * i + k) if flip else 3 * i + k] for k in range(3)]
+        a0 = t[0] * odd_m + t[1] * even + t[2] * odd
+        a1 = t[0] * even + t[1] * odd + t[2] * even_p
+        out0 = a0 if out0 is None else out0 + a0
+        out1 = a1 if out1 is None else out1 + a1
+    return out0, out1
+
+
+def attend_kernel(
+    tok_ref, mod_ref, mk_ref, owner_ref, wj_hbm,
+    xd_ref, fp_ref, mg_ref, qkv_ref, p_ref, ag_ref, ai_ref,
+    tokf, wj, ms, wsem, hs, hr, g_s, g_r, f_s, f_r, a_s, a_r, e_s, e_r,
+):
+    rows = tok_ref.shape[0]
+    width = tok_ref.shape[2]
+    half = width // 2
+    strips = lax.axis_size("strip")
+    chips = strips // 2
+    s = lax.axis_index("strip")
+    z = s // 2
+    c = lax.rem(s, 2)
+    sibling = 2 * z + 1 - c
+
+    wcopies = []
+    for part in range(3):
+        off = pl.multiple_of(part * width + c * half, 128)
+        cp = pltpu.make_async_copy(wj_hbm.at[:, pl.ds(off, half)], wj.at[part], wsem.at[part])
+        cp.start()
+        wcopies.append(cp)
+    strip_barrier(strips)
+
+    scale1 = spread(1.0 + mod_ref[:, width : 2 * width], width)
+    shift1 = spread(mod_ref[:, 0:width], width)
+
+    def first_row(r):
+        spread_columns(tokf, r, tok_ref[r].astype(F32))
+        for p in range(2):
+            x = every_second(tokf, r, p)
+            xd_ref[r, p] = x.astype(BF16)
+            n, _ = ln_parts(x)
+            fp_ref[r + 1, p] = (n * scale1 + shift1).astype(BF16)
+
+    first_row(0)
+    first_row(rows - 1)
+    up = rcopy(fp_ref.at[1], fp_ref.at[rows + 1], hs.at[0], hr.at[0], s - 1)
+    down = rcopy(fp_ref.at[rows], fp_ref.at[0], hs.at[1], hr.at[1], s + 1)
+
+    @pl.when(s > 0)
+    def _():
+        up.start()
+
+    @pl.when(s < strips - 1)
+    def _():
+        down.start()
+
+    def body(r, _):
+        first_row(r)
+        return 0
+
+    lax.fori_loop(1, rows - 1, body, 0)
+
+    def mixed_row(r):
+        for k in range(width // 128):
+            lanes = pl.ds(k * 128, 128)
+            weights = [mk_ref[t : t + 1, k * 128 : k * 128 + 128] for t in range(9)]
+            out = conv_row(
+                lambda i: (fp_ref[r + i, 0, :, lanes].astype(F32), fp_ref[r + i, 1, :, lanes].astype(F32)),
+                weights,
+                False,
+            )
+            for p in range(2):
+                ms[lax.rem(r, 2) * 2 + p, r // 2, :, lanes] = out[p].astype(BF16)
+
+    def body(r, _):
+        mixed_row(r)
+        return 0
+
+    lax.fori_loop(1, rows - 1, body, 0)
+
+    @pl.when(s > 0)
+    def _():
+        rcopy(fp_ref.at[1], fp_ref.at[0], hs.at[1], hr.at[1], s - 1).wait_recv()
+
+    @pl.when(s == 0)
+    def _():
+        fp_ref[0] = jnp.zeros_like(fp_ref[0])
+
+    mixed_row(0)
+
+    @pl.when(s < strips - 1)
+    def _():
+        rcopy(fp_ref.at[1], fp_ref.at[rows + 1], hs.at[0], hr.at[0], s + 1).wait_recv()
+
+    @pl.when(s == strips - 1)
+    def _():
+        fp_ref[rows + 1] = jnp.zeros_like(fp_ref[rows + 1])
+
+    mixed_row(rows - 1)
+
+    gathers = []
+    for d in range(1, chips):
+        g = lax.rem(z + d, chips)
+        cp = rcopy(ms.at[g], mg_ref.at[s], g_s.at[d], g_r.at[d], 2 * g + c)
+        cp.start()
+        gathers.append(cp)
+    mg_ref[s] = ms[z]
+    forwards = []
+    for d in range(chips):
+        i = 2 * lax.rem(z - d + chips, chips) + c
+        if d:
+            rcopy(ms.at[z], mg_ref.at[i], g_s.at[d], g_r.at[d], i).wait_recv()
+        cp = rcopy(mg_ref.at[i], mg_ref.at[i], f_s.at[d], f_r.at[d], sibling)
+        cp.start()
+        forwards.append(cp)
+    for d in range(chips):
+        i = 2 * lax.rem(z - d + chips, chips) + 1 - c
+        rcopy(mg_ref.at[i], mg_ref.at[i], f_s.at[d], f_r.at[d], sibling).wait_recv()
+
+    for part in range(3):
+        wcopies[part].wait()
+
+    def project(t, _):
+        x = mg_ref[pl.ds(2 * t, 2)].reshape(128, width)
+        for part in range(3):
+            y = jnp.dot(x, wj[part], preferred_element_type=F32).astype(BF16)
+            for n in range(3):
+                qkv_ref[3 * part + n, pl.ds(pl.multiple_of(t * 128, 128), 128), :] = y[:, n * 128 : n * 128 + 128]
+        return 0
+
+    lax.fori_loop(0, chips, project, 0)
+
+    total = strips * 64
+    where = lax.broadcasted_iota(jnp.int32, (1, total), 1)
+    lefts = lax.rem(where, 16) < 8
+    key_owner = jnp.zeros((1, total), jnp.int32)
+    for t in range(4):
+        both = jnp.where(lefts, owner_ref[2 * t], owner_ref[2 * t + 1])
+        key_owner = jnp.where(where // 128 == t, both, key_owner)
+    qleft = lax.rem(lax.broadcasted_iota(jnp.int32, (128, 1), 0), 16) < 8
+    lane = lax.broadcasted_iota(jnp.int32, (128, 128), 1) < 64
+    factor = 64 ** -0.5
+    sends = []
+    for n in range(3):
+        mine = c * 3 + n
+
+        def attend(t, _):
+            rws = pl.ds(pl.multiple_of(t * 128, 128), 128)
+            owner = jnp.where(qleft, owner_ref[2 * t], owner_ref[2 * t + 1])
+            allowed = owner == key_owner
+            q2 = qkv_ref[n, rws, :]
+            keys = qkv_ref[3 + n]
+            values = qkv_ref[6 + n]
+            outs = []
+            for h in range(2):
+                q = jnp.where(lane if h == 0 else jnp.logical_not(lane), q2, jnp.zeros_like(q2))
+                scores = lax.dot_general(q, keys, NT, preferred_element_type=F32) * factor
+                scores = jnp.where(allowed, scores, MASKED)
+                peak = jnp.max(scores, axis=-1, keepdims=True)
+                lifted = jnp.exp(scores - peak)
+                inv = 1.0 / jnp.sum(lifted, axis=-1, keepdims=True)
+                probs = (lifted * inv).astype(BF16)
+                p_ref[n, h, rws, :] = probs
+                outs.append(jnp.dot(probs, values, preferred_element_type=F32))
+            ag_ref[mine, rws, :] = jnp.where(lane, outs[0], outs[1]).astype(BF16)
+            return 0
+
+        lax.fori_loop(0, 4, attend, 0)
+        cp = rcopy(ag_ref.at[mine], ag_ref.at[mine], e_s.at[n], e_r.at[n], sibling)
+        cp.start()
+        sends.append(cp)
+        for d in range(1, strips):
+            t = lax.rem(s + d, strips)
+            cp = rcopy(
+                ag_ref.at[mine, pl.ds(pl.multiple_of(t * 64, 64), 64)],
+                ai_ref.at[mine, z],
+                a_s.at[n, d],
+                a_r.at[n, d],
+                t,
+            )
+            cp.start()
+            sends.append(cp)
+        ai_ref[mine, z] = ag_ref[mine, pl.ds(pl.multiple_of(s * 64, 64), 64), :]
+
+    for n in range(3):
+        other = (1 - c) * 3 + n
+        rcopy(ag_ref.at[other], ag_ref.at[other], e_s.at[n], e_r.at[n], sibling).wait_recv()
+        for d in range(1, strips):
+            i = lax.rem(s - d + strips, strips)
+            spot = lax.rem(i, 2) * 3 + n
+            rcopy(
+                ag_ref.at[spot, pl.ds(0, 64)], ai_ref.at[spot, i // 2], a_s.at[n, d], a_r.at[n, d], i
+            ).wait_recv()
+    for cp in gathers + forwards + sends:
+        cp.wait_send()
+
+    @pl.when(s > 0)
+    def _():
+        up.wait_send()
+
+    @pl.when(s < strips - 1)
+    def _():
+        down.wait_send()
+
+
+def attend(tokens, mod, mixer, owner, joint_weight, strips):
+    rows, cols, width = tokens.shape
+    chips = strips // 2
+    dma = pltpu.SemaphoreType.DMA
+    return pl.pallas_call(
+        attend_kernel,
+        name="attend_forward",
+        out_shape=(
+            jax.ShapeDtypeStruct((rows, 2, 16, width), BF16),
+            jax.ShapeDtypeStruct((rows + 2, 2, 16, width), BF16),
+            jax.ShapeDtypeStruct((strips, rows // 2, 16, width), BF16),
+            jax.ShapeDtypeStruct((9, strips * 64, 128), BF16),
+            jax.ShapeDtypeStruct((3, 2, strips * 64, strips * 64), BF16),
+            jax.ShapeDtypeStruct((6, strips * 64, 128), BF16),
+            jax.ShapeDtypeStruct((6, chips, 64, 128), BF16),
+        ),
+        in_specs=[WHOLE, WHOLE, WHOLE, SCALARS, LEFT],
+        out_specs=(WHOLE,) * 7,
+        scratch_shapes=[
+            pltpu.VMEM((rows, width // 128, cols, 128), F32),
+            pltpu.VMEM((3, width, width // 2), BF16),
+            pltpu.VMEM((chips, rows // 2, 16, width), BF16),
+            dma((3,)),
+            dma((2,)),
+            dma((2,)),
+            dma((chips,)),
+            dma((chips,)),
+            dma((chips,)),
+            dma((chips,)),
+            dma((3, strips)),
+            dma((3, strips)),
+            dma((3,)),
+            dma((3,)),
+        ],
+        compiler_params=pltpu.CompilerParams(
+            collective_id=0, has_side_effects=True, vmem_limit_bytes=VMEM_BYTES
+        ),
+    )(tokens, mod, mixer, owner, joint_weight)
+
+
+def gelu_both(x):
+    k0 = math.sqrt(2.0 / math.pi)
+    square = x * x
+    t = jnp.tanh(k0 * x * (1.0 + 0.044715 * square))
+    cdf = 0.5 + 0.5 * t
+    slope = cdf + (0.5 * k0) * x * (1.0 - t * t) * (1.0 + (3.0 * 0.044715) * square)
+    return x * cdf, slope
+
+
+def fold(x):
+    return x[0:8] + x[8:16]
+
+
+def ffn_kernel(
+    xd_ref, mod_ref, ai_ref, wo_ref, ob_ref, eb_ref, hk_ref, rb_ref, cot_ref, we_hbm, wr_hbm,
+    out_ref, rg_ref, og_ref, rw_ref, ew_ref, hkg_ref, mg_ref, sb_ref,
+    we, wr, tg, sc, ex, cg, act, agr, eg, b2, sg, b2_in, sg_in, res, b1, ctd, cotf, acc,
+    wsem, x_s, x_r, h_s, h_r, k_s, k_r,
+):
+    rows, _, width = cot_ref.shape
+    chip_rows = 2 * rows
+    blocks = rows * 2
+    piece = we.shape[2]
+    strips = lax.axis_size("strip")
+    chips = strips // 2
+    s = lax.axis_index("strip")
+    z = s // 2
+    c = lax.rem(s, 2)
+    sibling = 2 * z + 1 - c
+
+    def weight_copies(n):
+        off = pl.multiple_of((2 * n + c) * piece, 128)
+        return (
+            pltpu.make_async_copy(we_hbm.at[:, pl.ds(off, piece)], we.at[n], wsem.at[0, n]),
+            pltpu.make_async_copy(wr_hbm.at[pl.ds(off, piece)], wr.at[n], wsem.at[1, n]),
+        )
+
+    for n in range(chips):
+        for cp in weight_copies(n):
+            cp.start()
+    strip_barrier(strips)
+
+    def block_mod(n):
+        return spread(mod_ref[:, n * width : (n + 1) * width], width)
+
+    acc[...] = jnp.zeros_like(acc)
+    gate2 = block_mod(5)
+
+    def upstream_row(r, _):
+        spread_columns(cotf, r, cot_ref[r].astype(F32))
+        for p in range(2):
+            up = every_second(cotf, r, p)
+            ctd[2 * r + p] = up.astype(BF16)
+            two = (up * gate2).astype(BF16)
+            tg[c, 2 * r + p] = two
+            acc[0] += two.astype(F32)
+        return 0
+
+    lax.fori_loop(0, rows, upstream_row, 0)
+    tg_copy = rcopy(tg.at[c], tg.at[c], x_s.at[0], x_r.at[0], sibling)
+    tg_copy.start()
+
+    gate1 = block_mod(2)
+    shift2 = block_mod(3)
+    scale2 = 1.0 + block_mod(4)
+    bias1 = ob_ref[...]
+
+    def project(g, _):
+        x = jnp.concatenate([ai_ref[n, g] for n in range(6)], axis=-1)
+        y = jnp.dot(x, wo_ref[...], preferred_element_type=F32) + bias1
+        for r2 in range(rows // 2):
+            rp = 4 * r2 + g
+            branch = y[r2 * 16 : r2 * 16 + 16]
+            b1[rp] = branch
+            v = xd_ref[rp // 2, lax.rem(rp, 2)].astype(F32) + gate1 * branch
+            res[rp] = v
+            n, _ = ln_parts(v)
+            sc[c, rp] = (n * scale2 + shift2).astype(BF16)
+        return 0
+
+    lax.fori_loop(0, 4, project, 0)
+    sc_copy = rcopy(sc.at[c], sc.at[c], x_s.at[1], x_r.at[1], sibling)
+    sc_copy.start()
+
+    def up_copy(buffer, k, n):
+        return rcopy(
+            buffer.at[n, 1], buffer.at[n, chip_rows + 1], h_s.at[k, 0, n], h_r.at[k, 0, n], s - 2
+        )
+
+    def down_copy(buffer, k, n):
+        return rcopy(
+            buffer.at[n, chip_rows], buffer.at[n, 0], h_s.at[k, 1, n], h_r.at[k, 1, n], s + 2
+        )
+
+    def send_halo(buffer, k, n):
+        @pl.when(z > 0)
+        def _():
+            up_copy(buffer, k, n).start()
+
+        @pl.when(z < chips - 1)
+        def _():
+            down_copy(buffer, k, n).start()
+
+    def take_halo(buffer, k, n):
+        @pl.when(z > 0)
+        def _():
+            rcopy(
+                buffer.at[n, 1], buffer.at[n, 0], h_s.at[k, 1, n], h_r.at[k, 1, n], s - 2
+            ).wait_recv()
+
+        @pl.when(z == 0)
+        def _():
+            buffer[n, 0] = jnp.zeros_like(buffer[n, 0])
+
+        @pl.when(z < chips - 1)
+        def _():
+            rcopy(
+                buffer.at[n, 1], buffer.at[n, chip_rows + 1], h_s.at[k, 0, n], h_r.at[k, 0, n], s + 2
+            ).wait_recv()
+
+        @pl.when(z == chips - 1)
+        def _():
+            buffer[n, chip_rows + 1] = jnp.zeros_like(buffer[n, 0])
+
+    def drain_halo(buffer, k, n):
+        @pl.when(z > 0)
+        def _():
+            up_copy(buffer, k, n).wait_send()
+
+        @pl.when(z < chips - 1)
+        def _():
+            down_copy(buffer, k, n).wait_send()
+
+    sc_copy.wait_recv()
+    tiles = chip_rows // 4
+
+    def chip_tile(buffer, t):
+        return buffer[t // 2, pl.ds(lax.rem(t, 2) * 8, 8)].reshape(128, width)
+
+    def expand(n, _):
+        for cp in weight_copies(n):
+            cp.wait()
+        bias = eb_ref[2 * n + c]
+        for t in range(tiles):
+            y = jnp.dot(chip_tile(sc, t), we[n], preferred_element_type=F32) + bias
+            ex[n, pl.ds(1 + 4 * t, 4)] = y.astype(BF16).reshape(4, 2, 16, piece)
+        send_halo(ex, 0, n)
+        return 0
+
+    lax.fori_loop(0, chips, expand, 0)
+    tg_copy.wait_recv()
+    for cp in (tg_copy, sc_copy):
+        cp.wait_send()
+
+    def activate(n, _):
+        take_halo(ex, 0, n)
+        for t in range(tiles):
+            agr[pl.ds(8 * t, 8)] = lax.dot_general(
+                chip_tile(tg, t), wr[n], NT, preferred_element_type=F32
+            ).reshape(8, 16, piece)
+
+        def row(r, _):
+            for k in range(piece // 128):
+                lanes = pl.ds(k * 128, 128)
+                weights = [hk_ref[2 * n + c, t : t + 1, lanes] for t in range(9)]
+                out = conv_row(
+                    lambda i: (ex[n, r + i, 0, :, lanes].astype(F32), ex[n, r + i, 1, :, lanes].astype(F32)),
+                    weights,
+                    False,
+                )
+                for p in range(2):
+                    value, slope = gelu_both(out[p])
+                    act[2 * r + p, :, lanes] = value.astype(BF16)
+                    cg[n, r + 1, p, :, lanes] = (agr[2 * r + p, :, lanes] * slope).astype(BF16)
+            return 0
+
+        lax.fori_loop(0, chip_rows, row, 0)
+        send_halo(cg, 1, n)
+        full = act[...].reshape(chip_rows * 32, piece)
+        for t in range(tiles):
+            y = jnp.dot(full[t * 128 : t * 128 + 128], wr[n], preferred_element_type=F32)
+            y = y.reshape(8, 16, width)
+            spot = (t // 2, pl.ds((t % 2) * 8, 8))
+
+            @pl.when(n == 0)
+            def _():
+                b2[spot] = y
+
+            @pl.when(n > 0)
+            def _():
+                b2[spot] += y
+
+        rw_ref[n] = lax.dot_general(
+            full, tg[...].reshape(chip_rows * 32, width), TN, preferred_element_type=F32
+        ).astype(BF16)
+        return 0
+
+    hkg_ref[...] = jnp.zeros_like(hkg_ref)
+    lax.fori_loop(0, chips, activate, 0)
+    b2_copy = rcopy(b2.at[1 - c], b2_in, x_s.at[2], x_r.at[2], sibling)
+    b2_copy.start()
+
+    def backward(n, _):
+        take_halo(cg, 1, n)
+        for k in range(piece // 128):
+            lanes = pl.ds(k * 128, 128)
+            weights = [hk_ref[2 * n + c, t : t + 1, lanes] for t in range(9)]
+
+            def row(r, sums):
+                out = conv_row(
+                    lambda i: (cg[n, r + i, 0, :, lanes].astype(F32), cg[n, r + i, 1, :, lanes].astype(F32)),
+                    weights,
+                    True,
+                )
+                low = [out[p].astype(BF16) for p in range(2)]
+                for p in range(2):
+                    eg[2 * r + p, :, lanes] = low[p]
+                g0 = cg[n, r + 1, 0, :, lanes].astype(F32)
+                g1 = cg[n, r + 1, 1, :, lanes].astype(F32)
+                new = []
+                for i in range(3):
+                    even = ex[n, r + i, 0, :, lanes].astype(F32)
+                    odd = ex[n, r + i, 1, :, lanes].astype(F32)
+                    odd_m, even_p = shifts(even, odd)
+                    new.append(sums[3 * i] + fold(odd_m * g0 + even * g1))
+                    new.append(sums[3 * i + 1] + fold(even * g0 + odd * g1))
+                    new.append(sums[3 * i + 2] + fold(odd * g0 + even_p * g1))
+                new.append(sums[9] + fold(low[0].astype(F32) + low[1].astype(F32)))
+                return tuple(new)
+
+            sums = lax.fori_loop(
+                0, chip_rows, row, tuple(jnp.zeros((8, 128), F32) for _ in range(10))
+            )
+            for t in range(10):
+                hkg_ref[n, t : t + 1, lanes] = jnp.sum(sums[t], axis=0, keepdims=True)
+        full = eg[...].reshape(chip_rows * 32, piece)
+        for t in range(tiles):
+            y = lax.dot_general(
+                full[t * 128 : t * 128 + 128], we[n], NT, preferred_element_type=F32
+            )
+            y = y.reshape(8, 16, width)
+            spot = (t // 2, pl.ds((t % 2) * 8, 8))
+
+            @pl.when(n == 0)
+            def _():
+                sg[spot] = y
+
+            @pl.when(n > 0)
+            def _():
+                sg[spot] += y
+
+        ew_ref[n] = lax.dot_general(
+            sc[...].reshape(chip_rows * 32, width), full, TN, preferred_element_type=F32
+        ).astype(BF16)
+        return 0
+
+    lax.fori_loop(0, chips, backward, 0)
+    sg_copy = rcopy(sg.at[1 - c], sg_in, x_s.at[3], x_r.at[3], sibling)
+    sg_copy.start()
+    b2_copy.wait_recv()
+    sg_copy.wait_recv()
+    bias2 = rb_ref[...]
+
+    def finish(r, _):
+        for p in range(2):
+            rp = 2 * r + p
+            grad = sg[c, rp] + sg_in[rp]
+            v = res[rp]
+            n, inv = ln_parts(v)
+            branch = b1[rp]
+            up = ctd[rp].astype(F32)
+            acc[1] += grad
+            acc[2] += grad * n
+            inner = grad * scale2
+            mean0 = jnp.mean(inner, axis=-1, keepdims=True)
+            mean1 = jnp.mean(inner * n, axis=-1, keepdims=True)
+            total = up + inv * (inner - mean0 - n * mean1)
+            rg_ref[rp] = total
+            acc[3] += total * branch
+            one = (total * gate1).astype(BF16)
+            og_ref[lax.rem(rp, 4), rp // 4] = one
+            acc[4] += one.astype(F32)
+            branch2 = b2[c, rp] + b2_in[rp] + bias2
+            acc[5] += up * branch2
+            y = v + gate2 * branch2
+            for k in range(width // 128):
+                cotf[r, k, pl.ds(p, 16, stride=2), :] = y[:, k * 128 : k * 128 + 128]
+        out_ref[r] = jnp.concatenate(
+            [cotf[r, k] for k in range(width // 128)], axis=-1
+        ).astype(BF16)
+        return 0
+
+    lax.fori_loop(0, rows, finish, 0)
+
+    def halves(x):
+        return jnp.concatenate(
+            [jnp.sum(x[0:8], axis=0, keepdims=True), jnp.sum(x[8:16], axis=0, keepdims=True)], axis=0
+        )
+
+    mg_ref[0] = halves(acc[3])
+    mg_ref[1] = halves(acc[1])
+    mg_ref[2] = halves(acc[2])
+    mg_ref[3] = halves(acc[5])
+    sb_ref[0:1] = jnp.sum(acc[0], axis=0, keepdims=True)
+    sb_ref[1:2] = jnp.sum(acc[4], axis=0, keepdims=True)
+
+    def drain(n, _):
+        drain_halo(ex, 0, n)
+        drain_halo(cg, 1, n)
+        return 0
+
+    lax.fori_loop(0, chips, drain, 0)
+    b2_copy.wait_send()
+    sg_copy.wait_send()
+
+
+def feed_forward(xd, mod, ai, wo, ob, eb, hk, rb, cot, we, wr, strips):
+    rows, cols, width = cot.shape
+    chips = strips // 2
+    hidden = we.shape[1]
+    piece = hidden // strips
+    dma = pltpu.SemaphoreType.DMA
+    chip_rows = 2 * rows
+    blocks = 2 * rows
+    shape = jax.ShapeDtypeStruct
+    return pl.pallas_call(
+        ffn_kernel,
+        name="feed_forward",
+        out_shape=(
+            shape((rows, cols, width), BF16),
+            shape((blocks, 16, width), F32),
+            shape((4, rows // 2, 16, width), BF16),
+            shape((chips, piece, width), BF16),
+            shape((chips, width, piece), BF16),
+            shape((chips, 16, piece), F32),
+            shape((4, 2, width), F32),
+            shape((2, width), F32),
+        ),
+        in_specs=[WHOLE] * 9 + [LEFT] * 2,
+        out_specs=(WHOLE,) * 8,
+        scratch_shapes=[
+            pltpu.VMEM((chips, width, piece), BF16),
+            pltpu.VMEM((chips, piece, width), BF16),
+            pltpu.VMEM((2, blocks, 16, width), BF16),
+            pltpu.VMEM((2, blocks, 16, width), BF16),
+            pltpu.VMEM((chips, chip_rows + 2, 2, 16, piece), BF16),
+            pltpu.VMEM((chips, chip_rows + 2, 2, 16, piece), BF16),
+            pltpu.VMEM((2 * blocks, 16, piece), BF16),
+            pltpu.VMEM((2 * blocks, 16, piece), F32),
+            pltpu.VMEM((2 * blocks, 16, piece), BF16),
+            pltpu.VMEM((2, blocks, 16, width), F32),
+            pltpu.VMEM((2, blocks, 16, width), F32),
+            pltpu.VMEM((blocks, 16, width), F32),
+            pltpu.VMEM((blocks, 16, width), F32),
+            pltpu.VMEM((blocks, 16, width), F32),
+            pltpu.VMEM((blocks, 16, width), F32),
+            pltpu.VMEM((blocks, 16, width), BF16),
+            pltpu.VMEM((rows, width // 128, cols, 128), F32),
+            pltpu.VMEM((6, 16, width), F32),
+            dma((2, chips)),
+            dma((4,)),
+            dma((4,)),
+            dma((2, 2, chips)),
+            dma((2, 2, chips)),
+            dma((2,)),
+            dma((2,)),
+        ],
+        compiler_params=pltpu.CompilerParams(
+            collective_id=1, has_side_effects=True, vmem_limit_bytes=VMEM_BYTES
+        ),
+    )(xd, mod, ai, wo, ob, eb, hk, rb, cot, we, wr)
+
+
+def attend_back_kernel(
+    og_ref, qkv_ref, p_ref, ag_ref, mg_ref, fp_ref, xd_ref, rg_ref, mod_ref, mk_ref, wo_ref, wj_hbm,
+    tg_ref, jo_ref, mkg_ref, m1_ref,
+    wj, gg, da, ds, dqkv, mp, mp_in, md, mr, mo, fg, tkf, acc,
+    wsem, g_s, g_r, f_s, f_r, p_s, p_r, b_s, b_r, hs, hr,
+):
+    rows, cols, width = tg_ref.shape
+    half = width // 2
+    strips = lax.axis_size("strip")
+    chips = strips // 2
+    s = lax.axis_index("strip")
+    z = s // 2
+    c = lax.rem(s, 2)
+    sibling = 2 * z + 1 - c
+    total = strips * 64
+
+    wcopies = []
+    for part in range(3):
+        off = pl.multiple_of(part * width + c * half, 128)
+        cp = pltpu.make_async_copy(wj_hbm.at[:, pl.ds(off, half)], wj.at[part], wsem.at[part])
+        cp.start()
+        wcopies.append(cp)
+    strip_barrier(strips)
+
+    gathers = []
+    for d in range(1, chips):
+        g = lax.rem(z + d, chips)
+        cp = rcopy(og_ref.at[g], gg.at[s], g_s.at[d], g_r.at[d], 2 * g + c)
+        cp.start()
+        gathers.append(cp)
+    gg[s] = og_ref[z]
+    forwards = []
+    for d in range(chips):
+        i = 2 * lax.rem(z - d + chips, chips) + c
+        if d:
+            rcopy(og_ref.at[z], gg.at[i], g_s.at[d], g_r.at[d], i).wait_recv()
+        cp = rcopy(gg.at[i], gg.at[i], f_s.at[d], f_r.at[d], sibling)
+        cp.start()
+        forwards.append(cp)
+    for d in range(chips):
+        i = 2 * lax.rem(z - d + chips, chips) + 1 - c
+        rcopy(gg.at[i], gg.at[i], f_s.at[d], f_r.at[d], sibling).wait_recv()
+
+    wo_own = wo_ref[pl.ds(pl.multiple_of(c * half, 128), half), :]
+
+    def attended_grad(t, _):
+        x = gg[pl.ds(2 * t, 2)].reshape(128, width)
+        y = lax.dot_general(x, wo_own, NT, preferred_element_type=F32).astype(BF16)
+        for n in range(3):
+            da[n, pl.ds(pl.multiple_of(t * 128, 128), 128), :] = y[:, n * 128 : n * 128 + 128]
+        return 0
+
+    lax.fori_loop(0, chips, attended_grad, 0)
+
+    lane = lax.broadcasted_iota(jnp.int32, (128, 128), 1) < 64
+    lanes_all = lax.broadcasted_iota(jnp.int32, (total, 128), 1) < 64
+    factor = 64 ** -0.5
+    for n in range(3):
+
+        def tile(t, _):
+            rws = pl.ds(pl.multiple_of(t * 128, 128), 128)
+            d2 = da[n, rws, :]
+            keys = qkv_ref[3 + n]
+            values = qkv_ref[6 + n]
+            outs = []
+            for h in range(2):
+                dh = jnp.where(lane if h == 0 else jnp.logical_not(lane), d2, jnp.zeros_like(d2))
+                dp = lax.dot_general(dh, values, NT, preferred_element_type=F32)
+                probs = p_ref[n, h, rws, :].astype(F32)
+                inner = jnp.sum(probs * dp, axis=-1, keepdims=True)
+                grad = (probs * (dp - inner)).astype(BF16)
+                ds[h, rws, :] = grad
+                outs.append(jnp.dot(grad, keys, preferred_element_type=F32))
+            dqkv[n, rws, :] = (jnp.where(lane, outs[0], outs[1]) * factor).astype(BF16)
+            return 0
+
+        lax.fori_loop(0, 4, tile, 0)
+        q2 = qkv_ref[n]
+        d2 = da[n]
+        dk = [lax.dot_general(ds[h], q2, TN, preferred_element_type=F32) for h in range(2)]
+        dqkv[3 + n] = (jnp.where(lanes_all, dk[0], dk[1]) * factor).astype(BF16)
+        dv = [lax.dot_general(p_ref[n, h], d2, TN, preferred_element_type=F32) for h in range(2)]
+        dqkv[6 + n] = jnp.where(lanes_all, dv[0], dv[1]).astype(BF16)
+
+    for part in range(3):
+        wcopies[part].wait()
+
+    def joined(part, rws):
+        return jnp.concatenate([dqkv[3 * part + n, rws, :] for n in range(3)], axis=-1)
+
+    def partial(core):
+        def body(i, _):
+            rws = pl.ds(pl.multiple_of((2 * i + core) * 64, 64), 64)
+            y = None
+            for part in range(3):
+                w = lax.dot_general(joined(part, rws), wj[part], NT, preferred_element_type=F32)
+                y = w if y is None else y + w
+            mp[core, i] = y
+            return 0
+
+        lax.fori_loop(0, chips, body, 0)
+
+    partial(1 - c)
+    mp_copy = rcopy(mp.at[1 - c], mp_in, p_s.at[0], p_r.at[0], sibling)
+    mp_copy.start()
+    partial(c)
+    mp_copy.wait_recv()
+    backs = []
+    for d in range(chips):
+        i = lax.rem(z + d, chips)
+        low = (mp[c, i] + mp_in[i]).astype(BF16).reshape(rows // 2, 16, width)
+        if d:
+            mo[i] = low
+            cp = rcopy(mo.at[i], mr.at[z], b_s.at[d], b_r.at[d], 2 * i + c)
+            cp.start()
+            backs.append(cp)
+        else:
+            mr[z] = low
+
+    def joint_grad(part, _):
+        x = mg_ref[...].reshape(total, width)
+        y = lax.dot_general(x, joined(part, slice(None)), TN, preferred_element_type=F32)
+        jo_ref[part] = y.astype(BF16).reshape(jo_ref.shape[1:])
+        return 0
+
+    lax.fori_loop(0, 3, joint_grad, 0)
+    own = gg[:, :, :, pl.ds(pl.multiple_of(c * half, 128), half)].reshape(total, half)
+    full = jnp.concatenate([ag_ref[n] for n in range(6)], axis=-1)
+    y = lax.dot_general(full, own, TN, preferred_element_type=F32)
+    jo_ref[3] = y.astype(BF16).reshape(jo_ref.shape[1:])
+
+    for d in range(1, chips):
+        i = lax.rem(z - d + chips, chips)
+        rcopy(mo.at[i], mr.at[i], b_s.at[d], b_r.at[d], 2 * i + c).wait_recv()
+    for r in (0, rows - 1):
+        for p in range(2):
+            md[r + 1, p] = mr[(r % 2) * 2 + p, r // 2]
+    up = rcopy(md.at[1], md.at[rows + 1], hs.at[0], hr.at[0], s - 1)
+    down = rcopy(md.at[rows], md.at[0], hs.at[1], hr.at[1], s + 1)
+
+    @pl.when(s > 0)
+    def _():
+        up.start()
+
+    @pl.when(s < strips - 1)
+    def _():
+        down.start()
+
+    for r in range(1, rows - 1):
+        for p in range(2):
+            md[r + 1, p] = mr[(r % 2) * 2 + p, r // 2]
+
+    acc[...] = jnp.zeros_like(acc)
+    scale1 = spread(1.0 + mod_ref[:, width : 2 * width], width)
+
+    def finish_row(r):
+        for k in range(width // 128):
+            lanes = pl.ds(k * 128, 128)
+            weights = [mk_ref[t : t + 1, k * 128 : k * 128 + 128] for t in range(9)]
+            out = conv_row(
+                lambda i: (md[r + i, 0, :, lanes].astype(F32), md[r + i, 1, :, lanes].astype(F32)),
+                weights,
+                True,
+            )
+            fg[0, :, lanes] = out[0]
+            fg[1, :, lanes] = out[1]
+            g0 = md[r + 1, 0, :, lanes].astype(F32)
+            g1 = md[r + 1, 1, :, lanes].astype(F32)
+            for i in range(3):
+                even = fp_ref[r + i, 0, :, lanes].astype(F32)
+                odd = fp_ref[r + i, 1, :, lanes].astype(F32)
+                odd_m, even_p = shifts(even, odd)
+                acc[3 * i, :, lanes] += odd_m * g0 + even * g1
+                acc[3 * i + 1, :, lanes] += even * g0 + odd * g1
+                acc[3 * i + 2, :, lanes] += odd * g0 + even_p * g1
+        for p in range(2):
+            rp = 2 * r + p
+            grad = fg[p]
+            n, inv = ln_parts(xd_ref[r, p].astype(F32))
+            acc[9] += grad
+            acc[10] += grad * n
+            inner = grad * scale1
+            mean0 = jnp.mean(inner, axis=-1, keepdims=True)
+            mean1 = jnp.mean(inner * n, axis=-1, keepdims=True)
+            y = rg_ref[rp] + inv * (inner - mean0 - n * mean1)
+            for k in range(width // 128):
+                tkf[r, k, pl.ds(p, 16, stride=2), :] = y[:, k * 128 : k * 128 + 128]
+        tg_ref[r] = jnp.concatenate([tkf[r, k] for k in range(width // 128)], axis=-1)
+
+    def body(r, _):
+        finish_row(r)
+        return 0
+
+    lax.fori_loop(1, rows - 1, body, 0)
+
+    @pl.when(s > 0)
+    def _():
+        rcopy(md.at[1], md.at[0], hs.at[1], hr.at[1], s - 1).wait_recv()
+
+    @pl.when(s == 0)
+    def _():
+        md[0] = jnp.zeros_like(md[0])
+
+    finish_row(0)
+
+    @pl.when(s < strips - 1)
+    def _():
+        rcopy(md.at[1], md.at[rows + 1], hs.at[0], hr.at[0], s + 1).wait_recv()
+
+    @pl.when(s == strips - 1)
+    def _():
+        md[rows + 1] = jnp.zeros_like(md[0])
+
+    finish_row(rows - 1)
+
+    mkg_ref[...] = jnp.zeros_like(mkg_ref)
+    for t in range(9):
+        mkg_ref[t : t + 1] = jnp.sum(acc[t], axis=0, keepdims=True)
+
+    def halves(x):
+        return jnp.concatenate(
+            [jnp.sum(x[0:8], axis=0, keepdims=True), jnp.sum(x[8:16], axis=0, keepdims=True)], axis=0
+        )
+
+    m1_ref[0] = halves(acc[9])
+    m1_ref[1] = halves(acc[10])
+    for cp in gathers + forwards + backs + [mp_copy]:
+        cp.wait_send()
+
+    @pl.when(s > 0)
+    def _():
+        up.wait_send()
+
+    @pl.when(s < strips - 1)
+    def _():
+        down.wait_send()
+
+
+def attend_back(og, qkv, probs, ag, mg, fp, xd, rg, mod, mk, wo, wj, strips):
+    rows, _, _, width = xd.shape
+    chips = strips // 2
+    total = strips * 64
+    half = width // 2
+    dma = pltpu.SemaphoreType.DMA
+    shape = jax.ShapeDtypeStruct
+    return pl.pallas_call(
+        attend_back_kernel,
+        name="attend_backward",
+        out_shape=(
+            shape((rows, 32, width), F32),
+            shape((4, chips, 2, 2, width // chips // 4, half), BF16),
+            shape((16, width), F32),
+            shape((2, 2, width), F32),
+        ),
+        in_specs=[WHOLE] * 11 + [LEFT],
+        out_specs=(WHOLE,) * 4,
+        scratch_shapes=[
+            pltpu.VMEM((3, width, half), BF16),
+            pltpu.VMEM((strips, rows // 2, 16, width), BF16),
+            pltpu.VMEM((3, total, 128), BF16),
+            pltpu.VMEM((2, total, total), BF16),
+            pltpu.VMEM((9, total, 128), BF16),
+            pltpu.VMEM((2, chips, 64, width), F32),
+            pltpu.VMEM((chips, 64, width), F32),
+            pltpu.VMEM((rows + 2, 2, 16, width), BF16),
+            pltpu.VMEM((4, rows // 2, 16, width), BF16),
+            pltpu.VMEM((4, rows // 2, 16, width), BF16),
+            pltpu.VMEM((2, 16, width), F32),
+            pltpu.VMEM((rows, width // 128, 32, 128), F32),
+            pltpu.VMEM((11, 16, width), F32),
+            dma((3,)),
+            dma((chips,)),
+            dma((chips,)),
+            dma((chips,)),
+            dma((chips,)),
+            dma((1,)),
+            dma((1,)),
+            dma((chips,)),
+            dma((chips,)),
+            dma((2,)),
+            dma((2,)),
+        ],
+        compiler_params=pltpu.CompilerParams(
+            collective_id=2, has_side_effects=True, vmem_limit_bytes=VMEM_BYTES
+        ),
+    )(og, qkv, probs, ag, mg, fp, xd, rg, mod, mk, wo, wj)
+
+
+def bcopy(src, dst, send, recv, batch, strip):
+    return pltpu.make_async_remote_copy(
+        src_ref=src, dst_ref=dst, send_sem=send, recv_sem=recv,
+        device_id=(batch, strip), device_id_type=MESH,
+    )
+
+
+def block_barrier(strips):
+    s = lax.axis_index("strip")
+    b = lax.axis_index("batch")
+    z = s // 2
+    barrier = pltpu.get_barrier_semaphore()
+    count = 0
+    for d in range(1, strips):
+        pl.semaphore_signal(
+            barrier, inc=1, device_id=(b, lax.rem(s + d, strips)), device_id_type=MESH
+        )
+        count += 1
+    for e in range(1, 4):
+        for core in range(2):
+            pl.semaphore_signal(
+                barrier, inc=1, device_id=(lax.rem(b + e, 4), 2 * z + core), device_id_type=MESH
+            )
+            count += 1
+    pl.semaphore_wait(barrier, count)
+
+
+def reduce_kernel(
+    rw_ref, ew_ref, jo_ref,
+    rout_ref, eout_ref, jout_ref, oout_ref,
+    r_in1, r_s1, r_in2, r_s2, r_in3, r_all,
+    e_in1, e_s1, e_in2, e_s2, e_in3, e_all,
+    a_in1, a_s1, a_in2, a_s2, a_in3, a_all,
+    b_in1, b_s1, b_in2, b_s2, b_in3, b_all,
+    s1s, s1r, s2s, s2r, s3s, s3r, s4s, s4r,
+):
+    strips = lax.axis_size("strip")
+    chips = strips // 2
+    s = lax.axis_index("strip")
+    b = lax.axis_index("batch")
+    z = s // 2
+    c = lax.rem(s, 2)
+    y, x = b // 2, lax.rem(b, 2)
+    x_mate = 2 * y + 1 - x
+    y_mate = 2 * (1 - y) + x
+    block_barrier(strips)
+
+    parts = [
+        (0, lambda t, q: rw_ref.at[t, :, q], r_in1, r_s1, r_in2, r_s2, r_in3),
+        (1, lambda t, q: ew_ref.at[:, t, q], e_in1, e_s1, e_in2, e_s2, e_in3),
+        (0, lambda t, q: jo_ref.at[pl.ds(0, 2), t, :, q], a_in1, a_s1, a_in2, a_s2, a_in3),
+        (1, lambda t, q: jo_ref.at[pl.ds(2, 2), t, q], b_in1, b_s1, b_in2, b_s2, b_in3),
+    ]
+    order = [1, 2, 3, 0]
+
+    def mates(first):
+        return (x, x_mate, y, y_mate) if first == 0 else (y, y_mate, x, x_mate)
+
+    def step1(k, d):
+        first, pick, in1 = parts[k][:3]
+        mine, mate, _, _ = mates(first)
+        t = lax.rem(z + d, chips)
+        return bcopy(pick(t, 1 - mine), in1.at[t], s1s.at[k, d], s1r.at[k, d], mate, s)
+
+    def step2(k, d):
+        first, _, _, s1, in2 = parts[k][:5]
+        _, _, other, mate = mates(first)
+        t = lax.rem(z + d, chips)
+        lead = (lambda q: s1.at[t, q]) if k == 0 else (lambda q: s1.at[t, :, q])
+        return bcopy(lead(1 - other), in2.at[t], s2s.at[k, d], s2r.at[k, d], mate, s), lead, other
+
+    def step3(k, d):
+        _, _, _, _, _, s2, in3 = parts[k]
+        t = lax.rem(z + d, chips)
+        return bcopy(s2.at[t], in3.at[d], s3s.at[k, d], s3r.at[k, d], b, 2 * t + c)
+
+    for k in range(4):
+        for d in order:
+            step1(k, d).start()
+    for d in order:
+        t = lax.rem(z + d, chips)
+        for k in range(4):
+            first, pick, in1, s1 = parts[k][:4]
+            mine = mates(first)[0]
+            step1(k, d).wait_recv()
+            own = pick(t, mine)
+            for i in range(2 if k != 1 else 4):
+                s1[t, i] = (own[i].astype(F32) + in1[t, i].astype(F32)).astype(BF16)
+            step2(k, d)[0].start()
+    for d in order:
+        t = lax.rem(z + d, chips)
+        for k in range(4):
+            s2, in2 = parts[k][5], parts[k][4]
+            cp, lead, other = step2(k, d)
+            cp.wait_recv()
+            s2[t] = (lead(other)[...].astype(F32) + in2[t].astype(F32)).astype(BF16)
+            if d:
+                step3(k, d).start()
+    alls = [r_all, e_all, a_all, b_all]
+
+    def step4(k, e):
+        dest = lax.rem(b + e, 4)
+        if k == 0:
+            return bcopy(alls[0].at[b], alls[0].at[b], s4s.at[k, e], s4r.at[k, e, c], dest, s)
+        return bcopy(
+            alls[k].at[2, 0], alls[k].at[x, c], s4s.at[k, e], s4r.at[k, e, c], dest, 2 * z + y
+        )
+
+    for k in range(4):
+        s2, in3 = parts[k][5], parts[k][6]
+        v = s2[z].astype(F32)
+        for d in range(1, chips):
+            step3(k, d).wait_recv()
+            v = v + in3[d].astype(F32)
+        if k == 0:
+            alls[k][b] = v.astype(BF16)
+        else:
+            alls[k][2, 0] = v.astype(BF16)
+
+            @pl.when(c == y)
+            def _():
+                alls[k][x, c] = v.astype(BF16)
+
+        for e in range(1, 4):
+            step4(k, e).start()
+        if k:
+
+            @pl.when(c != y)
+            def _():
+                step4(k, 0).start()
+
+    for e in range(1, 4):
+        step4(0, e).wait_recv()
+    for q in range(4):
+        n = r_all.shape[1]
+        rout_ref[q * n : q * n + n] = r_all[q].astype(F32)
+    for k in range(1, 4):
+        for xs in range(2):
+            for cs in range(2):
+                source = 2 * c + xs
+                e = lax.rem(b - source + 4, 4)
+                local = jnp.logical_and(source == b, cs == c)
+
+                @pl.when(jnp.logical_not(local))
+                def _():
+                    bcopy(
+                        alls[k].at[xs, cs], alls[k].at[xs, cs], s4s.at[k, e], s4r.at[k, e, cs],
+                        source, 2 * z + cs,
+                    ).wait_recv()
+
+                rows = slice(xs * 48, xs * 48 + 48)
+                half = alls[k].shape[-1]
+                if k == 1:
+                    for n in range(4):
+                        at = pl.multiple_of((2 * n + cs) * half, 128)
+                        eout_ref[rows, pl.ds(at, half)] = alls[1][xs, cs, n].astype(F32)
+                elif k == 2:
+                    for n in range(2):
+                        at = (2 * n + cs) * half
+                        jout_ref[rows, at : at + half] = alls[2][xs, cs, n].astype(F32)
+                else:
+                    at = (4 + cs) * half
+                    jout_ref[rows, at : at + half] = alls[3][xs, cs, 0].astype(F32)
+                    oout_ref[rows, cs * half : cs * half + half] = alls[3][xs, cs, 1].astype(F32)
+    for k in range(4):
+        for d in order:
+            step1(k, d).wait_send()
+            step2(k, d)[0].wait_send()
+            if d:
+                step3(k, d).wait_send()
+        for e in range(1, 4):
+            step4(k, e).wait_send()
+        if k:
+
+            @pl.when(c != y)
+            def _():
+                step4(k, 0).wait_send()
+
+
+def reduce_weights(rw, ew, jo, strips):
+    chips = strips // 2
+    dma = pltpu.SemaphoreType.DMA
+    shape = jax.ShapeDtypeStruct
+    vm = pltpu.VMEM
+
+    def buffers(n, m, lanes, lead):
+        full = (chips,) + lead
+        return full
+
+    half = ew.shape[-1]
+    hidden = 8 * half
+    width = 2 * half
+    r = [
+        vm((chips, 2, 96, width), BF16),
+        vm((chips, 2, 96, width), BF16),
+        vm((chips, 96, width), BF16),
+        vm((chips, 96, width), BF16),
+        vm((chips, 96, width), BF16),
+        vm((4, 96, width), BF16),
+    ]
+
+    def cols(n):
+        return [
+            vm((chips, n, 2, 48, half), BF16),
+            vm((chips, n, 2, 48, half), BF16),
+            vm((chips, n, 48, half), BF16),
+            vm((chips, n, 48, half), BF16),
+            vm((chips, n, 48, half), BF16),
+            vm((3, 2, n, 48, half), BF16),
+        ]
+
+    return pl.pallas_call(
+        reduce_kernel,
+        name="reduce_weights",
+        out_shape=(
+            shape((384, width), F32),
+            shape((96, hidden), F32),
+            shape((96, 3 * width), F32),
+            shape((96, width), F32),
+        ),
+        in_specs=[WHOLE] * 3,
+        out_specs=(WHOLE,) * 4,
+        scratch_shapes=r + cols(4) + cols(2) + cols(2) + [dma((4, 4))] * 7 + [dma((4, 4, 2))],
+        compiler_params=pltpu.CompilerParams(
+            collective_id=3, has_side_effects=True, vmem_limit_bytes=VMEM_BYTES
+        ),
+    )(rw, ew, jo)
+
+
+def tail_kernel(
+    hkg_ref, mkg_ref, sb_ref, m1_ref, m4_ref, silu_ref, slope_ref, label_ref, slot_ref, aw_hbm,
+    ag_ref, tab_ref, ab_ref, sm_ref,
+    pieces, arrived, summed, amod, aw,
+    wsem, s1s, s1r, s2s, s2r, m1s, m1r, m2s, m2r, m3s, m3r,
+):
+    strips = lax.axis_size("strip")
+    chips = strips // 2
+    s = lax.axis_index("strip")
+    b = lax.axis_index("batch")
+    z = s // 2
+    c = lax.rem(s, 2)
+    sibling = 2 * z + 1 - c
+    width = m1_ref.shape[-1]
+    own = width // strips
+    weights = pltpu.make_async_copy(
+        aw_hbm.at[pl.ds(pl.multiple_of(s * own, 16), own)], aw, wsem.at[0]
+    )
+    weights.start()
+    block_barrier(strips)
+
+    rows = [m1_ref[0], m1_ref[1], m4_ref[0], m4_ref[1], m4_ref[2], m4_ref[3]]
+    rows.append(jnp.zeros((4, width), F32))
+    amod[b, s] = jnp.concatenate(rows, axis=0).astype(BF16)
+    copies = []
+    for e in range(1, 4):
+        cp = bcopy(
+            amod.at[b, s], amod.at[b, s], m1s.at[e], m1r.at[e], lax.rem(b + e, 4), s
+        )
+        cp.start()
+        copies.append(cp)
+
+    pad = jnp.zeros((16, 128 - own), F32)
+    biases = jnp.concatenate([mkg_ref[0:9], sb_ref[1:2], sb_ref[0:1], mkg_ref[11:16]], axis=0)
+    for t in range(strips):
+        hidden = jnp.where(c == t % 2, hkg_ref[t // 2], 0.0)
+        piece = jnp.concatenate([hidden, biases[:, t * own : t * own + own], pad], axis=1)
+        pieces[t] = piece.astype(BF16)
+    for d in range(1, strips):
+        t = lax.rem(s + d, strips)
+        cp = bcopy(pieces.at[t], arrived.at[d], s1s.at[d], s1r.at[d], b, t)
+        cp.start()
+        copies.append(cp)
+
+    def batch_wait(e):
+        i = lax.rem(b - e + 4, 4)
+        bcopy(amod.at[i, s], amod.at[i, s], m1s.at[e], m1r.at[e], i, s).wait_recv()
+
+    for e in range(1, 4):
+        batch_wait(e)
+    for d in range(1, chips):
+        t = 2 * lax.rem(z + d, chips) + c
+        cp = bcopy(amod.at[:, s], amod.at[:, s], m2s.at[d], m2r.at[d], b, t)
+        cp.start()
+        copies.append(cp)
+    for d in range(chips):
+        i = 2 * lax.rem(z - d + chips, chips) + c
+        if d:
+            bcopy(amod.at[:, i], amod.at[:, i], m2s.at[d], m2r.at[d], b, i).wait_recv()
+        cp = bcopy(amod.at[:, i], amod.at[:, i], m3s.at[d], m3r.at[d], b, sibling)
+        cp.start()
+        copies.append(cp)
+
+    total = pieces[s].astype(F32)
+    for d in range(1, strips):
+        bcopy(pieces.at[0], arrived.at[d], s1s.at[d], s1r.at[d], b, s).wait_recv()
+        total = total + arrived[d].astype(F32)
+    summed[b] = total.astype(BF16)
+    for e in range(1, 4):
+        cp = bcopy(summed.at[b], summed.at[b], s2s.at[e], s2r.at[e], lax.rem(b + e, 4), s)
+        cp.start()
+        copies.append(cp)
+
+    for d in range(chips):
+        i = 2 * lax.rem(z - d + chips, chips) + 1 - c
+        bcopy(amod.at[:, i], amod.at[:, i], m3s.at[d], m3r.at[d], b, sibling).wait_recv()
+
+    weights.wait()
+    count = 4 * strips * 16
+    slots = silu_ref.shape[0]
+    flat = amod[...].reshape(count, width)
+    column = lax.broadcasted_iota(jnp.int32, (slots, count), 1)
+    hit = lax.broadcasted_iota(jnp.int32, (slots, count), 0) == slot_ref[...]
+    silu_grad = jnp.zeros((slots, own), F32)
+    for m in range(6):
+        chosen = jnp.logical_and(hit, lax.rem(column, 16) // 2 == m)
+        chosen = jnp.where(chosen, 1.0, 0.0).astype(BF16)
+        grad = jnp.dot(chosen, flat, preferred_element_type=F32)
+        ab_ref[m : m + 1] = jnp.sum(grad, axis=0, keepdims=True)
+        low = grad.astype(BF16)
+        lanes = slice(m * width, m * width + width)
+        ag_ref[:, lanes] = lax.dot_general(silu_ref[...], low, TN, preferred_element_type=F32)
+        silu_grad = silu_grad + lax.dot_general(low, aw[:, lanes], NT, preferred_element_type=F32)
+    grad = silu_grad * slope_ref[...]
+    classes = tab_ref.shape[1]
+    onehot = lax.broadcasted_iota(jnp.int32, (slots, classes), 1) == label_ref[...]
+    tab_ref[...] = lax.dot_general(
+        grad, jnp.where(onehot, 1.0, 0.0), TN,
+        precision=lax.Precision.HIGHEST, preferred_element_type=F32,
+    )
+
+    total = summed[b].astype(F32)
+    for e in range(1, 4):
+        i = lax.rem(b - e + 4, 4)
+        bcopy(summed.at[i], summed.at[i], s2s.at[e], s2r.at[e], i, s).wait_recv()
+        total = total + summed[i].astype(F32)
+    sm_ref[...] = total
+    for cp in copies:
+        cp.wait_send()
+
+
+def tail(hkg, mkg, sb, m1, m4, silu, slope, labels, slot, aw, classes, strips):
+    width = m1.shape[-1]
+    chips = strips // 2
+    own = width // strips
+    dma = pltpu.SemaphoreType.DMA
+    shape = jax.ShapeDtypeStruct
+    return pl.pallas_call(
+        tail_kernel,
+        name="tail",
+        out_shape=(
+            shape((own, 6 * width), F32),
+            shape((own, classes), F32),
+            shape((6, width), F32),
+            shape((16, 512), F32),
+        ),
+        in_specs=[WHOLE] * 9 + [LEFT],
+        out_specs=(WHOLE,) * 4,
+        scratch_shapes=[
+            pltpu.VMEM((strips, 16, 512), BF16),
+            pltpu.VMEM((strips, 16, 512), BF16),
+            pltpu.VMEM((4, 16, 512), BF16),
+            pltpu.VMEM((4, strips, 16, width), BF16),
+            pltpu.VMEM((own, 6 * width), BF16),
+            dma((1,)),
+            dma((strips,)),
+            dma((strips,)),
+            dma((4,)),
+            dma((4,)),
+            dma((4,)),
+            dma((4,)),
+            dma((chips,)),
+            dma((chips,)),
+            dma((chips,)),
+            dma((chips,)),
+        ],
+        compiler_params=pltpu.CompilerParams(
+            collective_id=4, has_side_effects=True, vmem_limit_bytes=VMEM_BYTES
+        ),
+    )(hkg, mkg, sb, m1, m4, silu, slope, labels, slot, aw)
+
+
+def timestep_features(time_steps, model_width):
+    half_width = model_width // 2
+    frequencies = jnp.exp(
+        -math.log(10000.0) * jnp.arange(half_width, dtype=F32) / half_width
+    )
+    angles = time_steps.astype(F32)[..., None] * frequencies
+    return jnp.concatenate([jnp.cos(angles), jnp.sin(angles)], axis=-1)
+
+
+def local_grouped(
+    tokens, tile_owner, time_steps, class_labels, class_embedding_matrix, adaptive_weight,
+    adaptive_bias, mixer_kernel, joint_weight, output_weight, output_bias, expand_weight,
+    expand_bias, hidden_kernel, reduce_weight, reduce_bias, output_cotangent,
+):
+    _, rows, cols, width = tokens.shape
+    strips = lax.axis_size("strip")
+    s = lax.axis_index("strip")
+    classes = class_embedding_matrix.shape[1]
+    latents = time_steps.shape[1]
+    own = width // strips
+    piece = expand_weight.shape[1] // strips
+    owner = tile_owner[0].reshape(-1)
+
+    numbers = lax.all_gather(
+        jnp.concatenate([time_steps[0], class_labels[0], owner]), "batch", axis=0
+    )
+    onehot = (class_labels[0][:, None] == jnp.arange(classes, dtype=jnp.int32)).astype(BF16)
+    condition = timestep_features(time_steps[0], width) + jnp.einsum(
+        "bn,dn->bd", onehot, class_embedding_matrix, preferred_element_type=F32
+    )
+    silu_cond = jax.nn.silu(condition).astype(BF16)
+    modulation = jnp.dot(silu_cond, adaptive_weight, preferred_element_type=F32)
+    modulation = modulation + adaptive_bias.astype(F32)
+    pair = lax.dynamic_slice_in_dim(owner, 2 * (s * rows // (strips * rows // 4)), 2)
+    mod = jnp.dot(
+        (pair[:, None] == jnp.arange(latents, dtype=jnp.int32)).astype(F32),
+        modulation,
+        precision=lax.Precision.HIGHEST,
+    )
+    mixer = mixer_kernel.T.astype(F32)
+    hidden = hidden_kernel.T.astype(F32).reshape(9, strips, piece).transpose(1, 0, 2)
+
+    xd, fp, mg, qkv, probs, ag, ai = attend(tokens[0], mod, mixer, owner, joint_weight, strips)
+    out, rg, og, rw, ew, hkg, m4, sb = feed_forward(
+        xd, mod, ai, output_weight, output_bias.astype(F32)[None],
+        expand_bias.astype(F32).reshape(strips, 1, piece), hidden,
+        reduce_bias.astype(F32)[None], output_cotangent[0], expand_weight, reduce_weight, strips,
+    )
+    tg, jo, mkg, m1 = attend_back(
+        og, qkv, probs, ag, mg, fp, xd, rg, mod, mixer, output_weight, joint_weight, strips
+    )
+    chips = strips // 2
+    rout, eout, jout, oout = reduce_weights(
+        rw.reshape(chips, 2, 2, piece // 4, width),
+        ew.reshape(chips, chips, 2, 2, width // chips // 4, piece),
+        jo,
+        strips,
+    )
+
+    all_steps = numbers[:, :latents].reshape(-1)
+    all_labels = numbers[:, latents : 2 * latents].reshape(-1)
+    all_owner = numbers[:, 2 * latents :].reshape(4, 4, 2)
+    features = lax.dynamic_slice_in_dim(timestep_features(all_steps, width), s * own, own, 1)
+    all_hot = (all_labels[:, None] == jnp.arange(classes, dtype=jnp.int32)).astype(BF16)
+    table = lax.dynamic_slice_in_dim(class_embedding_matrix, s * own, own, 0)
+    all_condition = features + jnp.einsum("bn,dn->bd", all_hot, table, preferred_element_type=F32)
+    sigmoid = jax.nn.sigmoid(all_condition)
+    silu_own = (all_condition * sigmoid).astype(BF16)
+    slope = sigmoid * (1.0 + all_condition * (1.0 - sigmoid))
+    slot = all_owner + latents * jnp.arange(4, dtype=jnp.int32)[:, None, None]
+    slot = jnp.broadcast_to(slot[:, :, None, None, :], (4, 4, strips // 4, 8, 2)).reshape(1, -1)
+    adaptive, table_grad, bias, small = tail(
+        hkg, mkg, sb, m1, m4, silu_own, slope, all_labels[:, None], slot, adaptive_weight,
+        classes, strips,
+    )
+    bias = lax.dynamic_slice_in_dim(bias.reshape(-1), s * 6 * own, 6 * own)
+    return (
+        out[None],
+        tg[None],
+        table_grad,
+        adaptive,
+        bias,
+        small[:9, piece : piece + own].T,
+        jout,
+        oout,
+        small[9, piece : piece + own],
+        eout,
+        small[9, :piece],
+        small[:9, :piece].T,
+        rout,
+        small[10, piece : piece + own],
+    )
+
+
 EXACT_PRECISION = lax.Precision.HIGHEST
 
 
@@ -68,15 +1522,6 @@
         ]
         columns.append(jnp.sum(window * gradient, axis=(0, 1, 2)))
     return jnp.stack(columns, axis=1)
-
-
-def timestep_features(time_steps, model_width):
-    half_width = model_width // 2
-    frequencies = jnp.exp(
-        -math.log(10000.0) * jnp.arange(half_width, dtype=jnp.float32) / half_width
-    )
-    angles = time_steps.astype(jnp.float32)[..., None] * frequencies
-    return jnp.concatenate([jnp.cos(angles), jnp.sin(angles)], axis=-1)
 
 
 def group_owner(owner):
@@ -446,8 +1891,9 @@
 
 
 def solution(mesh):
+    grouped = (mesh.shape["batch"], mesh.shape["strip"]) == (4, 8)
     return jax.shard_map(
-        local,
+        local_grouped if grouped else local,
         mesh=mesh,
         in_specs=(
             P("batch", "strip", None, None),

time: 880 us -> 307 us (0.35)
  waiting for transfers between devices: 367 us -> 0 us
  Pallas kernels: 0 us -> 266 us
  local copies, waits for them, and re-layouts: 180 us -> 22.2 us
  matrix products: 133 us -> 6.31 us
  blocking collectives: 99.5 us -> 7.06 us
  other arithmetic: 56 us -> 3.27 us
  starting transfers between devices: 17.7 us -> 0 us
  between operations: 17.7 us -> 1.53 us
    pallas_call x0 -> x5, Pallas kernels: none -> 266 us  [the longest x1 100 us: reduce_weights(): pl.pallas_call(reduce_kernel, name='reduce_weights', out_shape=(shape((38...]
    reduce_scatter x6 -> x0, waiting for transfers between devices: 226 us -> none  [the longest x1 78.1 us: local(): lax.psum_scatter(adaptive_grad.astype(jnp.bfloat16), 'strip', scatter_dim...]
    dot_general x26 -> x3, matrix products: 133 us -> 6.31 us  [the longest x1 4.51 us: local_grouped(): modulation = jnp.dot(silu_cond, adaptive_weight, preferred_element_type=F32)]
    unnamed x15 -> x0, waiting for transfers between devices: 60.8 us -> none
    all_gather x2 -> x0, blocking collectives: 54.3 us -> none  [the longest x1 36.2 us: local(): lax.all_gather(log_total[..., 0], 'strip', axis=4, tiled=True)]
    all_gather x4 -> x0, waiting for transfers between devices: 45.6 us -> none  [the longest x1 25.3 us: local(): lax.all_gather(keys_local, 'strip', axis=1, tiled=True)]
    all_gather x4 -> x1, local copies, waits for them, and re-layouts: 35.2 us -> 0.08 us  [local_grouped(): lax.all_gather(jnp.concatenate([time_steps[0], class_labels[0], owner]),...]
    reshape x9 -> x2, local copies, waits for them, and re-layouts: 35.2 us -> 1.59 us  [the longest x1 0.87 us: local_grouped(): bias = lax.dynamic_slice_in_dim(bias.reshape(-1), s * 6 * own, 6 * own)]
  transfers between devices with their start and end apart: 21 -> 0, of which waited for: 12 -> 0; matrix products, arithmetic and copies ran while one was open for 28% -> 0% of each run, Pallas kernels for 0% -> 0%
where the time goes in v1:
time: 307 us; the launch traced here: 306 us
  Pallas kernels  266 us (87%)
  local copies, waits for them, and re-layouts  22.2 us (7%)
  blocking collectives  7.06 us (2%)
  matrix products  6.31 us (2%)
  other arithmetic  3.27 us (1%)
    pallas_call x1, Pallas kernels, reduce_weights(): pl.pallas_call(reduce_kernel, name='reduce_weights', out_shape=(shape((38...  100 us
    pallas_call x1, Pallas kernels, feed_forward(): pl.pallas_call(ffn_kernel, name='feed_forward', out_shape=(shape((rows, c...  51.1 us
    pallas_call x1, Pallas kernels, attend_back(): pl.pallas_call(attend_back_kernel, name='attend_backward', out_shape=(sha...  46.1 us
    pallas_call x1, Pallas kernels, attend(): pl.pallas_call(attend_kernel, name='attend_forward', out_shape=(jax.Shape...  39.8 us
    pallas_call x1, Pallas kernels, tail(): pl.pallas_call(tail_kernel, name='tail', out_shape=(shape((own, 6 * width...  28.6 us
    unnamed x46, local copies, waits for them, and re-layouts  11.6 us
    unnamed x1, blocking collectives  7.06 us

profile of v1, /device:TPU:0, one launch (start us, length us, event | category | flops | bytes accessed | tf_op | source)
XLA Modules:
  0.0 306.4 jit_solution(7755724437764589853)
XLA Ops:
  0.7 0.9 copy.35
  3.2 4.5 %convolution_add_fusion = f32[8,4608]{1,0:T(8,128)S(1)} fusion(bf16[768,4608]{1,0:T(8,128)(2,1)} %aw_hbm.1, f32[4608]{0:T(1024)S(1)} %convert_element_type.43, bf16[768,1000]{0,1:T(8,128)(2,1)S(1)} %copy-done, f32[8,384]{1,0:T(8,128)S(1)} %get-tuple-element.75, f32[8,384]{1,0:T(8,128)S(1)} %get-tuple-element.74, s32[8]{0:T(128)} %bitcast.45), kind=kOutput, calls=%fused_computation | convolution fusion | flops 68998976 | bytes 8804384 | tf_op jit(solution)/shard_map/dot_general | solution.py:1404
  7.8 0.9 fusion.6.mod_ref
  9.3 39.8 %attend_forward.1 = (bf16[8,2,16,768]{3,2,1,0:T(8,128)(2,1)}, bf16[10,2,16,768]{3,2,1,0:T(8,128)(2,1)}, bf16[8,4,16,768]{3,2,1,0:T(8,128)(2,1)}, bf16[9,512,128]...) custom-call(bf16[8,32,768]{2,1,0:T(8,128)(2,1)} %bitcast.41, ...), custom_call_target="tpu_custom_call" | custom-call | tf_op jit(solution)/shard_map/attend_forward/pallas_call | solution.py:295
  51.7 51.1 %feed_forward.1 = (bf16[8,32,768]{2,1,0:T(8,128)(2,1)}, f32[16,16,768]{2,1,0:T(8,128)}, bf16[4,4,16,768]{3,2,1,0:T(8,128)(2,1)}, bf16[4,384,768]{2,1,0:T(8,128)(...) custom-call(bf16[8,2,16,768]{3,2,1,0:T(8,128)(2,1)} %get-tuple-element.41., ...), custom_call_target="tpu_custom_call" | custom-call | tf_op jit(solution)/shard_map/feed_forward/pallas_call | solution.py:656
  102.8 46.1 %attend_backward.1 = (f32[8,32,768]{2,1,0:T(8,128)}, bf16[4,4,2,2,48,384]{5,4,3,2,1,0:T(8,128)(2,1)}, f32[16,768]{1,0:T(8,128)}, f32[2,2,768]{2,1,0:T(2,128)}) custom-call(bf16[4,4,16,768]{3,2,1,0:T(8,128)(2,1)} %get-tuple-element.44.og_ref, bf16[9,512,128]{2,1,0:T(8,128)(2,1)} %get-tuple-element.45.qkv_ref, ...), custom_call_target="tpu_custom_call" | custom-call | tf_op jit(solution)/shard_map/attend_backward/pallas_call | solution.py:949
  149.0 100.3 %reduce_weights.1 = (f32[384,768]{1,0:T(8,128)}, f32[96,3072]{1,0:T(8,128)}, f32[96,2304]{1,0:T(8,128)}, f32[96,768]{1,0:T(8,128)}) custom-call(bf16[4,2,2,96,768]{4,3,2,1,0:T(8,128)(2,1)} %bitcast.34, bf16[4,4,2,2,48,384]{5,4,3,2,1,0:T(8,128)(2,1)} %bitcast.35, bf16[4,4,2,2,48,384]{5,4,3,2,1,0:T(8,128)(2,1)} %get-tuple-element.63.jo_ref), custom_call_target="tpu_custom_call" | custom-call | tf_op jit(solution)/shard_map/reduce_weights/pallas_call | solution.py:1203
  250.8 7.1 %all-reduce = s32[96]{0:T(128)S(1)} all-reduce(s32[96]{0:T(128)S(1)} %add_dynamic-update-slice_fusion), channel_id=2, replica_groups=mesh['batch'=4,'strip'=8] {'batch'}, use_global_device_ids=true, to_apply=%add | all-reduce | flops 96 | bytes 768
  258.4 0.9 add_multiply_fusion
  260.2 0.7 reshape.87.slot_ref
  261.0 28.6 %tail.1 = (f32[96,4608]{1,0:T(8,128)}, f32[96,1000]{1,0:T(8,128)}, f32[6,768]{1,0:T(8,128)}, f32[16,512]{1,0:T(8,128)}) custom-call(f32[4,16,384]{2,1,0:T(8,128)} %get-tuple-element.52.hkg_ref, f32[16,768]{1,0:T(8,128)} %get-tuple-element.53.mkg_ref, f32[2,768]{1,0:T(2,128)} %get-tuple-element.54.sb_ref, f32[2,2,768]{2,1,0:T(2,128)} %get-tuple-element.55.m1_ref, ...), custom_call_target="tpu_custom_call" | custom-call | tf_op jit(solution)/shard_map/tail/pallas_call | solution.py:1338
  289.6 0.9 reshape.88
  291.2 1.3 slice_bitcast_fusion
  292.5 1.3 slice_bitcast_fusion.1
  293.8 1.3 slice_reduce_fusion
  295.1 1.3 slice_bitcast_fusion.2
  296.4 1.8 copy.52
  298.1 2.1 copy.53
  300.2 0.7 copy.54
  301.0 1.2 copy.55
  302.7 0.9 copy.56
  303.7 0.7 copy.57
  304.4 1.0 copy.58
  305.4 1.0 copy.59
  (63 shorter events, 8.4 us)
Async XLA Ops:
  0.6 2.6 copy-start
  1.6 6.1 %copy-start.10 = (s32[8]{0:T(128)}, s32[8]{0:T(128)S(1)}, u32[]{:S(2)}) copy-start(s32[8]{0:T(128)S(1)} %reshape_squeeze.3.owner_ref) | copy-start | bytes 100
  3.2 5.4 %copy-start.8 = (bf16[768,9]{0,1:T(8,128)(2,1)S(1)}, bf16[768,9]{0,1:T(8,128)(2,1)}, u32[]{:S(2)}) copy-start(bf16[768,9]{0,1:T(8,128)(2,1)} %param.24) | copy-start | bytes 41476
  9.3 39.8 %copy-start.7 = (bf16[3072,9]{0,1:T(8,128)(2,1)S(1)}, bf16[3072,9]{0,1:T(8,128)(2,1)}, u32[]{:S(2)}) copy-start(bf16[3072,9]{0,1:T(8,128)(2,1)} %param.30) | copy-start | bytes 165892
  9.3 40.6 %copy-start.9 = (bf16[3072]{0:T(1024)(128)(2,1)S(1)}, bf16[3072]{0:T(1024)(128)(2,1)}, u32[]{:S(2)}) copy-start(bf16[3072]{0:T(1024)(128)(2,1)} %param.29) | copy-start | bytes 18436
  9.3 41.2 %copy-start.12 = (bf16[768]{0:T(1024)(128)(2,1)S(1)}, bf16[768]{0:T(1024)(128)(2,1)}, u32[]{:S(2)}) copy-start(bf16[768]{0:T(1024)(128)(2,1)} %param.27) | copy-start | bytes 4612
  9.3 41.8 %copy-start.13 = (bf16[768]{0:T(1024)(128)(2,1)S(1)}, bf16[768]{0:T(1024)(128)(2,1)}, u32[]{:S(2)}) copy-start(bf16[768]{0:T(1024)(128)(2,1)} %param.32) | copy-start | bytes 4612
  148.9 100.4 %copy-start.16 = (u32[32]{0:T(128)S(1)}, u32[32]{0:T(128)}, u32[]{:S(2)}) copy-start(u32[32]{0:T(128)} %constant.51) | copy-start | bytes 388
  148.9 101.7 %copy-start.11 = (s32[8]{0:T(128)S(1)}, s32[8]{0:T(128)}, u32[]{:S(2)}) copy-start(s32[8]{0:T(128)} %copy-done.10) | copy-start | bytes 100
  148.9 101.6 %copy-start.14 = (s32[1,8]{1,0:T(1,128)S(1)}, s32[1,8]{1,0:T(1,128)}, u32[]{:S(2)}) copy-start(s32[1,8]{1,0:T(1,128)} %param.20) | copy-start | bytes 100
  148.9 101.6 %copy-start.15 = (s32[1,8]{1,0:T(1,128)S(1)}, s32[1,8]{1,0:T(1,128)}, u32[]{:S(2)}) copy-start(s32[1,8]{1,0:T(1,128)} %param.19) | copy-start | bytes 100
  289.6 11.3 %copy-start.1 = (f32[96,4608]{1,0:T(8,128)S(1)}, f32[96,4608]{1,0:T(8,128)}, u32[]{:S(2)}) copy-start(f32[96,4608]{1,0:T(8,128)} %get-tuple-element.96) | copy-start | bytes 5308420
  290.5 9.7 %copy-start.5 = (f32[96,1000]{1,0:T(8,128)S(1)}, f32[96,1000]{1,0:T(8,128)}, u32[]{:S(2)}) copy-start(f32[96,1000]{1,0:T(8,128)} %get-tuple-element.95) | copy-start | bytes 1152004
  301.0 1.8 copy-start.4
  301.0 2.7 copy-start.6
  302.7 1.6 copy-start.3
  303.7 1.7 copy-start.2

commit v2 on v0

--- a/solution.py
+++ b/solution.py
@@ -1,15 +1,1393 @@
 import math
+from types import SimpleNamespace
 
 import jax
 import jax.numpy as jnp
 from jax import lax
+from jax.experimental import pallas as pl
+from jax.experimental.pallas import tpu as pltpu
 from jax.sharding import PartitionSpec as P
 
 HEADS = 12
-
-
 EPSILON = 1e-06
 MASKED = -1e30
+MESH = pl.DeviceIdType.MESH
+F32 = jnp.float32
+BF16 = jnp.bfloat16
+VMEM_BYTES = 62 * 1024 * 1024
+WHOLE = pl.BlockSpec(memory_space=pltpu.VMEM)
+LEFT = pl.BlockSpec(memory_space=pl.ANY)
+SCALARS = pl.BlockSpec(memory_space=pltpu.SMEM)
+NT = (((1,), (1,)), ((), ()))
+TN = (((0,), (0,)), ((), ()))
+
+
+def dot(a, b):
+    return jnp.dot(a, b, preferred_element_type=F32)
+
+
+def dot_nt(a, b):
+    return lax.dot_general(a, b, NT, preferred_element_type=F32)
+
+
+def dot_tn(a, b):
+    return lax.dot_general(a, b, TN, preferred_element_type=F32)
+
+
+def send_to(src, dst, sems, index, batch, strip):
+    return pltpu.make_async_remote_copy(
+        src_ref=src,
+        dst_ref=dst,
+        send_sem=sems[0].at[index],
+        recv_sem=sems[1].at[index],
+        device_id=(batch, strip),
+        device_id_type=MESH,
+    )
+
+
+def entry_barrier(strips):
+    s = lax.axis_index("strip")
+    b = lax.axis_index("batch")
+    z = s // 2
+    barrier = pltpu.get_barrier_semaphore()
+    count = 0
+    for d in range(1, strips):
+        pl.semaphore_signal(
+            barrier, inc=1, device_id=(b, lax.rem(s + d, strips)), device_id_type=MESH
+        )
+        count += 1
+    for e in range(1, 4):
+        for core in range(2):
+            pl.semaphore_signal(
+                barrier, inc=1, device_id=(lax.rem(b + e, 4), 2 * z + core), device_id_type=MESH
+            )
+            count += 1
+    pl.semaphore_wait(barrier, count)
+
+
+def spread(mod, width):
+    return jnp.concatenate(
+        [jnp.broadcast_to(mod[0:1], (8, width)), jnp.broadcast_to(mod[1:2], (8, width))], axis=0
+    )
+
+
+def spread_columns(buffer, r, x):
+    for k in range(x.shape[-1] // 128):
+        buffer[r, k] = x[:, k * 128 : k * 128 + 128]
+
+
+def every_second(buffer, r, p):
+    return jnp.concatenate(
+        [buffer[r, k, pl.ds(p, 16, stride=2), :] for k in range(buffer.shape[1])], axis=-1
+    )
+
+
+def interleave(buffer, r, p, x):
+    for k in range(x.shape[-1] // 128):
+        buffer[r, k, pl.ds(p, 16, stride=2), :] = x[:, k * 128 : k * 128 + 128]
+
+
+def joined(buffer, r):
+    return jnp.concatenate([buffer[r, k] for k in range(buffer.shape[1])], axis=-1)
+
+
+def ln_parts(x):
+    centre = jnp.mean(x, axis=-1, keepdims=True)
+    centred = x - centre
+    var = jnp.mean(centred * centred, axis=-1, keepdims=True)
+    inv = lax.rsqrt(var + EPSILON)
+    return centred * inv, inv
+
+
+def ln_back(grad, n, inv):
+    mean0 = jnp.mean(grad, axis=-1, keepdims=True)
+    mean1 = jnp.mean(grad * n, axis=-1, keepdims=True)
+    return inv * (grad - mean0 - n * mean1)
+
+
+def window(load, r):
+    even = load(r, 0).astype(F32)
+    odd = load(r, 1).astype(F32)
+    n = even.shape[0]
+    j = lax.broadcasted_iota(jnp.int32, even.shape, 0)
+    odd_m = jnp.where(j == 0, 0.0, pltpu.roll(odd, 1, 0))
+    even_p = jnp.where(j == n - 1, 0.0, pltpu.roll(even, n - 1, 0))
+    return odd_m, even, odd, even_p
+
+
+def conv(rows, weights, flip):
+    out = []
+    for p in range(2):
+        total = None
+        for i in range(3):
+            for j in range(3):
+                t = 3 * i + j
+                a = weights[8 - t if flip else t] * rows[i][p + j]
+                total = a if total is None else total + a
+        out.append(total)
+    return out
+
+
+def taps(rows, centre, sums):
+    new = list(sums)
+    for i in range(3):
+        for j in range(3):
+            a = rows[i][j] * centre[0] + rows[i][1 + j] * centre[1]
+            t = 8 - (3 * i + j)
+            new[t] = sums[t] + (a[0:8] + a[8:16])
+    return new
+
+
+def halves(x):
+    return jnp.concatenate(
+        [jnp.sum(x[0:8], axis=0, keepdims=True), jnp.sum(x[8:16], axis=0, keepdims=True)], axis=0
+    )
+
+
+def gelu_both(x):
+    k0 = math.sqrt(2.0 / math.pi)
+    square = x * x
+    t = jnp.tanh(k0 * x * (1.0 + 0.044715 * square))
+    cdf = 0.5 + 0.5 * t
+    slope = cdf + (0.5 * k0) * x * (1.0 - t * t) * (1.0 + (3.0 * 0.044715) * square)
+    return x * cdf, slope
+
+
+def block_kernel(names, *refs):
+    m = SimpleNamespace(**dict(zip(names, refs)))
+    rows, cols, width = m.tok.shape
+    half = width // 2
+    strips = lax.axis_size("strip")
+    chips = strips // 2
+    chip_rows = 2 * rows
+    total = strips * 64
+    own = width // strips
+    s = lax.axis_index("strip")
+    b = lax.axis_index("batch")
+    z = s // 2
+    c = lax.rem(s, 2)
+    sibling = 2 * z + 1 - c
+    y, x = b // 2, lax.rem(b, 2)
+    x_mate = 2 * y + 1 - x
+    y_mate = 2 * (1 - y) + x
+    sent = []
+
+    def chip(d):
+        return lax.rem(z + d, chips)
+
+    def start(copy):
+        copy.start()
+        sent.append(copy)
+
+    loads = {}
+
+    def load(name, src, dst, index):
+        loads[name] = pltpu.make_async_copy(src, dst, m.load_sem.at[index])
+        loads[name].start()
+
+    for part in range(3):
+        off = pl.multiple_of(part * width + c * half, 128)
+        load(f"wj{part}", m.wj_hbm.at[:, pl.ds(off, half)], m.wj.at[part], part)
+    load("cot", m.cot_hbm, m.cot, 3)
+    load("wo", m.wo_hbm, m.wo, 4)
+    for n in range(chips):
+        off = pl.multiple_of((2 * n + c) * half, 128)
+        load(f"we{n}", m.we_hbm.at[:, pl.ds(off, half)], m.we.at[n], 5 + n)
+        load(f"wr{n}", m.wr_hbm.at[pl.ds(off, half)], m.wr.at[n], 5 + chips + n)
+    entry_barrier(strips)
+
+    m.cond_all[b] = m.cond[...]
+    for e in range(1, 4):
+        start(
+            send_to(m.cond_all.at[b], m.cond_all.at[b], m.cond_sem, e, lax.rem(b + e, 4), s)
+        )
+
+    def block_mod(n):
+        return spread(m.mod[:, n * width : (n + 1) * width], width)
+
+    scale1 = 1.0 + block_mod(1)
+    shift1 = block_mod(0)
+
+    def first_row(r):
+        spread_columns(m.rowf, r, m.tok[r].astype(F32))
+        for p in range(2):
+            v = every_second(m.rowf, r, p)
+            m.xd[r, p] = v.astype(BF16)
+            n, _ = ln_parts(v)
+            m.fp[r + 1, p] = (n * scale1 + shift1).astype(BF16)
+
+    def edge_sends(buffer, sems):
+        up = send_to(buffer.at[1], buffer.at[rows + 1], sems, 0, b, s - 1)
+        down = send_to(buffer.at[rows], buffer.at[0], sems, 1, b, s + 1)
+        return up, down
+
+    def start_edges(buffer, sems):
+        up, down = edge_sends(buffer, sems)
+
+        @pl.when(s > 0)
+        def _():
+            up.start()
+
+        @pl.when(s < strips - 1)
+        def _():
+            down.start()
+
+    def edges_sent(buffer, sems):
+        up, down = edge_sends(buffer, sems)
+
+        @pl.when(s > 0)
+        def _():
+            up.wait_send()
+
+        @pl.when(s < strips - 1)
+        def _():
+            down.wait_send()
+
+    def top_edge(buffer, sems):
+        @pl.when(s > 0)
+        def _():
+            send_to(buffer.at[1], buffer.at[0], sems, 1, b, s - 1).wait_recv()
+
+        @pl.when(s == 0)
+        def _():
+            buffer[0] = jnp.zeros_like(buffer[0])
+
+    def bottom_edge(buffer, sems):
+        @pl.when(s < strips - 1)
+        def _():
+            send_to(buffer.at[1], buffer.at[rows + 1], sems, 0, b, s + 1).wait_recv()
+
+        @pl.when(s == strips - 1)
+        def _():
+            buffer[rows + 1] = jnp.zeros_like(buffer[0])
+
+    first_row(0)
+    first_row(rows - 1)
+    start_edges(m.fp, m.fp_sem)
+
+    def body(r, _):
+        first_row(r)
+        return 0
+
+    lax.fori_loop(1, rows - 1, body, 0)
+
+    def mixed_rows(low, high):
+        for k in range(width // 128):
+            lanes = pl.ds(k * 128, 128)
+            weights = [m.mk[t : t + 1, k * 128 : k * 128 + 128] for t in range(9)]
+
+            def line(r, p):
+                return m.fp[r, p, :, lanes]
+
+            def step(r, carry):
+                new = window(line, r + 2)
+                out = conv((carry[0], carry[1], new), weights, False)
+                for p in range(2):
+                    m.ms[lax.rem(r, 2) * 2 + p, r // 2, :, lanes] = out[p].astype(BF16)
+                return carry[1], new
+
+            lax.fori_loop(low, high, step, (window(line, low), window(line, low + 1)))
+
+    mixed_rows(1, rows - 1)
+    top_edge(m.fp, m.fp_sem)
+    mixed_rows(0, 1)
+    bottom_edge(m.fp, m.fp_sem)
+    mixed_rows(rows - 1, rows)
+
+    def to_groups(source, target, sems, sems2):
+        for d in range(1, chips):
+            g = chip(d)
+            start(send_to(source.at[g], target.at[s], sems, d, b, 2 * g + c))
+        target[s] = source[z]
+
+    def pass_on(target, sems, sems2):
+        for d in range(chips):
+            i = 2 * chip(chips - d) + c
+            if d:
+                send_to(target.at[i], target.at[i], sems, d, b, i).wait_recv()
+            start(send_to(target.at[i], target.at[i], sems2, d, b, sibling))
+
+    def groups_ready(target, sems2):
+        for d in range(chips):
+            i = 2 * chip(chips - d) + 1 - c
+            send_to(target.at[i], target.at[i], sems2, d, b, sibling).wait_recv()
+
+    to_groups(m.ms, m.mg, m.mg_sem, m.mg_sem2)
+
+    m.acc[...] = jnp.zeros_like(m.acc)
+    gate2 = block_mod(5)
+    loads["cot"].wait()
+
+    def upstream_row(r, _):
+        spread_columns(m.rowf, r, m.cot[r].astype(F32))
+        for p in range(2):
+            up = every_second(m.rowf, r, p)
+            m.ctd[2 * r + p] = up.astype(BF16)
+            two = (up * gate2).astype(BF16)
+            m.tg[c, 2 * r + p] = two
+            m.acc[0] += two.astype(F32)
+        return 0
+
+    lax.fori_loop(0, rows, upstream_row, 0)
+    start(send_to(m.tg.at[c], m.tg.at[c], m.pair_sem, 0, b, sibling))
+
+    pass_on(m.mg, m.mg_sem, m.mg_sem2)
+    groups_ready(m.mg, m.mg_sem2)
+    for part in range(3):
+        loads[f"wj{part}"].wait()
+
+    def qkv_tile(t, _):
+        v = m.mg[pl.ds(2 * t, 2)].reshape(128, width)
+        for part in range(3):
+            w = dot(v, m.wj[part]).astype(BF16)
+            for n in range(3):
+                m.qkv[3 * part + n, pl.ds(pl.multiple_of(t * 128, 128), 128), :] = w[
+                    :, n * 128 : n * 128 + 128
+                ]
+        return 0
+
+    lax.fori_loop(0, chips, qkv_tile, 0)
+
+    where = lax.broadcasted_iota(jnp.int32, (1, total), 1)
+    lefts = lax.rem(where, 16) < 8
+    key_owner = jnp.zeros((1, total), jnp.int32)
+    for t in range(4):
+        both = jnp.where(lefts, m.owner[2 * t], m.owner[2 * t + 1])
+        key_owner = jnp.where(where // 128 == t, both, key_owner)
+    qleft = lax.rem(lax.broadcasted_iota(jnp.int32, (128, 1), 0), 16) < 8
+    lane = lax.broadcasted_iota(jnp.int32, (128, 128), 1) < 64
+    factor = 64 ** -0.5
+
+    def head(v, h):
+        return jnp.where(lane if h == 0 else jnp.logical_not(lane), v, jnp.zeros_like(v))
+
+    for n in range(3):
+        mine = c * 3 + n
+
+        def attend(t, _):
+            rws = pl.ds(pl.multiple_of(t * 128, 128), 128)
+            owner = jnp.where(qleft, m.owner[2 * t], m.owner[2 * t + 1])
+            allowed = owner == key_owner
+            q2 = m.qkv[n, rws, :]
+            keys = m.qkv[3 + n]
+            values = m.qkv[6 + n]
+            outs = []
+            for h in range(2):
+                scores = dot_nt(head(q2, h), keys) * factor
+                scores = jnp.where(allowed, scores, MASKED)
+                peak = jnp.max(scores, axis=-1, keepdims=True)
+                lifted = jnp.exp(scores - peak)
+                inv = 1.0 / jnp.sum(lifted, axis=-1, keepdims=True)
+                probs = (lifted * inv).astype(BF16)
+                m.probs[n, h, rws, :] = probs
+                outs.append(dot(probs, values))
+            m.ag[mine, rws, :] = jnp.where(lane, outs[0], outs[1]).astype(BF16)
+            return 0
+
+        lax.fori_loop(0, 4, attend, 0)
+        for d in range(1, strips):
+            t = lax.rem(s + d, strips)
+            start(
+                send_to(
+                    m.ag.at[mine, pl.ds(pl.multiple_of(t * 64, 64), 64)],
+                    m.ai.at[mine, z],
+                    m.ai_sem,
+                    (n, d),
+                    b,
+                    t,
+                )
+            )
+        start(send_to(m.ag.at[mine], m.ag.at[mine], m.ag_sem, n, b, sibling))
+        m.ai[mine, z] = m.ag[mine, pl.ds(pl.multiple_of(s * 64, 64), 64), :]
+
+    def chip_tile(buffer, t):
+        return buffer[t // 2, pl.ds((t % 2) * 8, 8)].reshape(128, width)
+
+    send_to(m.tg.at[c], m.tg.at[1 - c], m.pair_sem, 0, b, sibling).wait_recv()
+    for t in range(4):
+        m.tg_t[:, t * 128 : t * 128 + 128] = chip_tile(m.tg, t).T
+
+    for n in range(3):
+        for d in range(1, strips):
+            i = lax.rem(s - d + strips, strips)
+            spot = lax.rem(i, 2) * 3 + n
+            send_to(
+                m.ag.at[spot, pl.ds(0, 64)], m.ai.at[spot, i // 2], m.ai_sem, (n, d), b, i
+            ).wait_recv()
+
+    gate1 = block_mod(2)
+    shift2 = block_mod(3)
+    scale2 = 1.0 + block_mod(4)
+    loads["wo"].wait()
+
+    def project(g, _):
+        v = jnp.concatenate([m.ai[n, g] for n in range(6)], axis=-1)
+        w = dot(v, m.wo[...]) + m.ob[...]
+        for r2 in range(rows // 2):
+            rp = 4 * r2 + g
+            branch = w[r2 * 16 : r2 * 16 + 16]
+            m.b1[rp] = branch
+            u = m.xd[rp // 2, lax.rem(rp, 2)].astype(F32) + gate1 * branch
+            m.res[rp] = u
+            n, _ = ln_parts(u)
+            m.sc[c, rp] = (n * scale2 + shift2).astype(BF16)
+        return 0
+
+    lax.fori_loop(0, 4, project, 0)
+    start(send_to(m.sc.at[c], m.sc.at[c], m.pair_sem, 1, b, sibling))
+
+    def halo_sends(buffer, sems, n):
+        up = send_to(buffer.at[n, 1], buffer.at[n, chip_rows + 1], sems, (0, n), b, s - 2)
+        down = send_to(buffer.at[n, chip_rows], buffer.at[n, 0], sems, (1, n), b, s + 2)
+        return up, down
+
+    def start_halo(buffer, sems, n):
+        up, down = halo_sends(buffer, sems, n)
+
+        @pl.when(z > 0)
+        def _():
+            up.start()
+
+        @pl.when(z < chips - 1)
+        def _():
+            down.start()
+
+    def halo_sent(buffer, sems, n):
+        up, down = halo_sends(buffer, sems, n)
+
+        @pl.when(z > 0)
+        def _():
+            up.wait_send()
+
+        @pl.when(z < chips - 1)
+        def _():
+            down.wait_send()
+
+    def take_halo(buffer, sems, n):
+        @pl.when(z > 0)
+        def _():
+            send_to(buffer.at[n, 1], buffer.at[n, 0], sems, (1, n), b, s - 2).wait_recv()
+
+        @pl.when(z == 0)
+        def _():
+            buffer[n, 0] = jnp.zeros_like(buffer[n, 0])
+
+        @pl.when(z < chips - 1)
+        def _():
+            send_to(buffer.at[n, 1], buffer.at[n, chip_rows + 1], sems, (0, n), b, s + 2).wait_recv()
+
+        @pl.when(z == chips - 1)
+        def _():
+            buffer[n, chip_rows + 1] = jnp.zeros_like(buffer[n, 0])
+
+    send_to(m.sc.at[c], m.sc.at[1 - c], m.pair_sem, 1, b, sibling).wait_recv()
+    for n in range(chips):
+        loads[f"we{n}"].wait()
+        loads[f"wr{n}"].wait()
+
+    def expand(n, _):
+        bias = m.eb[2 * n + c]
+        for t in range(4):
+            w = dot(chip_tile(m.sc, t), m.we[n]) + bias
+            m.ex[n, pl.ds(1 + 4 * t, 4)] = w.astype(BF16).reshape(4, 2, 16, half)
+        start_halo(m.ex, m.ex_sem, n)
+        return 0
+
+    lax.fori_loop(0, chips, expand, 0)
+    for t in range(4):
+        m.sc_t[:, t * 128 : t * 128 + 128] = chip_tile(m.sc, t).T
+
+    def r_one(n):
+        return send_to(m.rw.at[n, :, 1 - x], m.r1.at[n], m.r1_sem, n, x_mate, s)
+
+    def r_two(n):
+        return send_to(m.r1.at[n, 1 - y], m.r2.at[n], m.r2_sem, n, y_mate, s)
+
+    def r_three(d):
+        n = chip(d)
+        return send_to(m.r2.at[n], m.r3.at[d], m.r3_sem, d, b, 2 * n + c)
+
+    def r_four(e):
+        return send_to(m.r_all.at[b], m.r_all.at[b], m.r4_sem, e, lax.rem(b + e, 4), s)
+
+    def r_half(n):
+        r_one(n).wait_recv()
+        for i in range(2):
+            m.r1[n, i] = (m.r1[n, i].astype(F32) + m.rw[n, i, x].astype(F32)).astype(BF16)
+        r_two(n).start()
+
+    def r_quarter():
+        for d in (1, 2, 3, 0):
+            n = chip(d)
+            r_two(n).wait_recv()
+            m.r2[n] = (m.r2[n].astype(F32) + m.r1[n, y].astype(F32)).astype(BF16)
+            if d:
+                r_three(d).start()
+
+    def r_sum():
+        v = m.r2[z].astype(F32)
+        for d in range(1, chips):
+            r_three(d).wait_recv()
+            v = v + m.r3[d].astype(F32)
+        m.r_all[b] = v.astype(BF16)
+        for e in range(1, 4):
+            r_four(e).start()
+
+    def by_x(j):
+        return isinstance(j, int) and j in (4, 6)
+
+    def c_source(j):
+        return m.ew.at[j] if not isinstance(j, int) or j < 4 else m.jo.at[j - 4]
+
+    def c_one(j):
+        if by_x(j):
+            return send_to(c_source(j).at[:, :, 1 - x], m.c1.at[j], m.c1_sem, j, x_mate, s)
+        return send_to(c_source(j).at[:, 1 - y], m.c1.at[j], m.c1_sem, j, y_mate, s)
+
+    def c_two(j):
+        if by_x(j):
+            return send_to(m.c1.at[j, :, 1 - y], m.c2.at[j], m.c2_sem, j, y_mate, s)
+        return send_to(m.c1.at[j, :, 1 - x], m.c2.at[j], m.c2_sem, j, x_mate, s)
+
+    def c_three(g, d):
+        t = chip(d)
+        return send_to(
+            m.c2.at[pl.ds(4 * g, 4), t], m.c3.at[g, d], m.c3_sem, (g, d), b, 2 * t + c
+        )
+
+    def c_four(g, e):
+        return pltpu.make_async_remote_copy(
+            src_ref=m.c_out.at[g],
+            dst_ref=m.c_all.at[g, x, c],
+            send_sem=m.c4_sem[0].at[g, e],
+            recv_sem=m.c4_sem[1].at[g, e, c],
+            device_id=(lax.rem(b + e, 4), 2 * z + y),
+            device_id_type=MESH,
+        )
+
+    def c_half(j):
+        c_one(j).wait_recv()
+        kept = c_source(j)[:, :, x] if by_x(j) else c_source(j)[:, y]
+        m.c1[j] = (m.c1[j].astype(F32) + kept.astype(F32)).astype(BF16)
+        c_two(j).start()
+
+    def c_quarter(g):
+        for j in range(4 * g, 4 * g + 4):
+            c_two(j).wait_recv()
+            kept = m.c1[j, :, y] if by_x(j) else m.c1[j, :, x]
+            m.c2[j] = (m.c2[j].astype(F32) + kept.astype(F32)).astype(BF16)
+        for d in range(1, chips):
+            c_three(g, d).start()
+
+    def c_sum(g):
+        v = [m.c2[4 * g + i, z].astype(F32) for i in range(4)]
+        for d in range(1, chips):
+            c_three(g, d).wait_recv()
+            for i in range(4):
+                v[i] = v[i] + m.c3[g, d, i].astype(F32)
+        for i in range(4):
+            m.c_out[g, i] = v[i].astype(BF16)
+
+        @pl.when(c == y)
+        def _():
+            m.c_all[g, x, c] = m.c_out[g]
+
+        for e in range(1, 4):
+            c_four(g, e).start()
+
+        @pl.when(c != y)
+        def _():
+            c_four(g, 0).start()
+
+    def activate(n, _):
+        take_halo(m.ex, m.ex_sem, n)
+        for t in range(4):
+            m.agr[pl.ds(8 * t, 8)] = dot_nt(chip_tile(m.tg, t), m.wr[n]).reshape(8, 16, half)
+        for k in range(half // 128):
+            lanes = pl.ds(k * 128, 128)
+            weights = [m.hk[2 * n + c, t : t + 1, lanes] for t in range(9)]
+
+            def line(r, p):
+                return m.ex[n, r, p, :, lanes]
+
+            def step(r, carry):
+                new = window(line, r + 2)
+                out = conv((carry[0], carry[1], new), weights, False)
+                for p in range(2):
+                    value, slope = gelu_both(out[p])
+                    m.act[2 * r + p, :, lanes] = value.astype(BF16)
+                    m.cg[n, r + 1, p, :, lanes] = (m.agr[2 * r + p, :, lanes] * slope).astype(BF16)
+                return carry[1], new
+
+            lax.fori_loop(0, chip_rows, step, (window(line, 0), window(line, 1)))
+        start_halo(m.cg, m.cg_sem, n)
+        full = m.act[...].reshape(total, half)
+        m.rw[n] = dot(m.tg_t[...], full).astype(BF16).reshape(m.rw.shape[1:])
+        r_one(n).start()
+        for t in range(4):
+            w = dot(full[t * 128 : t * 128 + 128], m.wr[n]).reshape(8, 16, width)
+            spot = (t // 2, pl.ds((t % 2) * 8, 8))
+
+            @pl.when(n == 0)
+            def _():
+                m.b2[spot] = w
+
+            @pl.when(n > 0)
+            def _():
+                m.b2[spot] += w
+
+        return 0
+
+    m.hkg[...] = jnp.zeros_like(m.hkg)
+    lax.fori_loop(0, chips, activate, 0)
+    start(send_to(m.b2.at[1 - c], m.b2_in, m.pair_sem, 2, b, sibling))
+
+    def backward(n, _):
+        take_halo(m.cg, m.cg_sem, n)
+        for k in range(half // 128):
+            lanes = pl.ds(k * 128, 128)
+            weights = [m.hk[2 * n + c, t : t + 1, lanes] for t in range(9)]
+
+            def line(r, p):
+                return m.cg[n, r, p, :, lanes]
+
+            def step(r, carry):
+                new = window(line, r + 2)
+                three = (carry[0], carry[1], new)
+                low = [v.astype(BF16) for v in conv(three, weights, True)]
+                for p in range(2):
+                    m.eg[2 * r + p, :, lanes] = low[p]
+                centre = [m.ex[n, r + 1, p, :, lanes].astype(F32) for p in range(2)]
+                sums = taps(three, centre, carry[2][:9])
+                both = low[0].astype(F32) + low[1].astype(F32)
+                sums.append(carry[2][9] + (both[0:8] + both[8:16]))
+                return carry[1], new, tuple(sums)
+
+            zeros = tuple(jnp.zeros((8, 128), F32) for _ in range(10))
+            _, _, sums = lax.fori_loop(
+                0, chip_rows, step, (window(line, 0), window(line, 1), zeros)
+            )
+            for t in range(10):
+                m.hkg[n, t : t + 1, lanes] = jnp.sum(sums[t], axis=0, keepdims=True)
+        full = m.eg[...].reshape(total, half)
+        for t in range(4):
+            w = dot_nt(full[t * 128 : t * 128 + 128], m.we[n]).reshape(8, 16, width)
+            spot = (t // 2, pl.ds((t % 2) * 8, 8))
+
+            @pl.when(n == 0)
+            def _():
+                m.sg[spot] = w
+
+            @pl.when(n > 0)
+            def _():
+                m.sg[spot] += w
+
+        m.ew[n] = dot(m.sc_t[...], full).astype(BF16).reshape(m.ew.shape[1:])
+        c_one(n).start()
+        r_half(n)
+        return 0
+
+    lax.fori_loop(0, chips, backward, 0)
+    start(send_to(m.sg.at[1 - c], m.sg_in, m.pair_sem, 3, b, sibling))
+    send_to(m.b2.at[c], m.b2_in, m.pair_sem, 2, b, sibling).wait_recv()
+    send_to(m.sg.at[c], m.sg_in, m.pair_sem, 3, b, sibling).wait_recv()
+
+    def finish(r, _):
+        for p in range(2):
+            rp = 2 * r + p
+            grad = m.sg[c, rp] + m.sg_in[rp]
+            v = m.res[rp]
+            n, inv = ln_parts(v)
+            branch = m.b1[rp]
+            up = m.ctd[rp].astype(F32)
+            m.acc[1] += grad
+            m.acc[2] += grad * n
+            back = up + ln_back(grad * scale2, n, inv)
+            m.rg[rp] = back
+            m.acc[3] += back * branch
+            one = (back * gate1).astype(BF16)
+            m.og[lax.rem(rp, 4), rp // 4] = one
+            m.acc[4] += one.astype(F32)
+            branch2 = m.b2[c, rp] + m.b2_in[rp] + m.rb[...]
+            m.acc[5] += up * branch2
+            interleave(m.rowf, r, p, v + gate2 * branch2)
+        m.out[r] = joined(m.rowf, r).astype(BF16)
+        return 0
+
+    lax.fori_loop(0, rows, finish, 0)
+    out_copy = pltpu.make_async_copy(m.out, m.out_hbm, m.load_sem.at[13])
+    out_copy.start()
+
+    to_groups(m.og, m.gg, m.gg_sem, m.gg_sem2)
+
+    pack = []
+    for v in (m.acc[3], m.acc[1], m.acc[2], m.acc[5]):
+        pair = halves(v)
+        for h in range(2):
+            pack += [pair[h : h + 1, 0:half], pair[h : h + 1, half:]]
+    m.late[b, s] = jnp.concatenate(pack, axis=0).astype(BF16)
+    for e in range(1, 4):
+        start(send_to(m.late.at[b, s], m.late.at[b, s], m.late_sem, e, lax.rem(b + e, 4), s))
+    sums_ob = jnp.sum(m.acc[4], axis=0, keepdims=True)
+    sums_rb = jnp.sum(m.acc[0], axis=0, keepdims=True)
+    pad_lanes = jnp.zeros((1, half - own), F32)
+    pad_rows = jnp.zeros((4, half), F32)
+    for t in range(strips):
+        piece = jnp.concatenate(
+            [
+                jnp.where(c == t % 2, m.hkg[t // 2, 0:10], 0.0),
+                jnp.concatenate([sums_ob[:, t * own : t * own + own], pad_lanes], axis=1),
+                jnp.concatenate([sums_rb[:, t * own : t * own + own], pad_lanes], axis=1),
+                pad_rows,
+            ],
+            axis=0,
+        )
+        m.piece[t] = piece.astype(BF16)
+    for d in range(1, strips):
+        t = lax.rem(s + d, strips)
+        start(send_to(m.piece.at[t], m.piece_in.at[d], m.piece_sem, d, b, t))
+
+    r_quarter()
+    c_half(0)
+    c_half(1)
+
+    pass_on(m.gg, m.gg_sem, m.gg_sem2)
+    groups_ready(m.gg, m.gg_sem2)
+    wo_own = m.wo[pl.ds(pl.multiple_of(c * half, 128), half), :]
+
+    def attended_grad(t, _):
+        v = m.gg[pl.ds(2 * t, 2)].reshape(128, width)
+        w = dot_nt(v, wo_own).astype(BF16)
+        for n in range(3):
+            m.da[n, pl.ds(pl.multiple_of(t * 128, 128), 128), :] = w[:, n * 128 : n * 128 + 128]
+        return 0
+
+    lax.fori_loop(0, chips, attended_grad, 0)
+
+    for n in range(3):
+        other = (1 - c) * 3 + n
+        send_to(m.ag.at[other], m.ag.at[other], m.ag_sem, n, b, sibling).wait_recv()
+    columns = m.gg[:, :, :, pl.ds(pl.multiple_of(c * half, 128), half)].reshape(total, half)
+    full = jnp.concatenate([m.ag[n] for n in range(6)], axis=-1)
+    m.jo[3] = dot_tn(full, columns).astype(BF16).reshape(m.jo.shape[1:])
+    c_one(7).start()
+
+    lanes_all = lax.broadcasted_iota(jnp.int32, (total, 128), 1) < 64
+    for n in range(3):
+
+        def tile(t, _):
+            rws = pl.ds(pl.multiple_of(t * 128, 128), 128)
+            d2 = m.da[n, rws, :]
+            keys = m.qkv[3 + n]
+            values = m.qkv[6 + n]
+            outs = []
+            for h in range(2):
+                dp = dot_nt(head(d2, h), values)
+                probs = m.probs[n, h, rws, :].astype(F32)
+                inner = jnp.sum(probs * dp, axis=-1, keepdims=True)
+                grad = (probs * (dp - inner)).astype(BF16)
+                m.ds[h, rws, :] = grad
+                outs.append(dot(grad, keys))
+            m.dqkv[n, rws, :] = (jnp.where(lane, outs[0], outs[1]) * factor).astype(BF16)
+            return 0
+
+        lax.fori_loop(0, 4, tile, 0)
+        q2 = m.qkv[n]
+        d2 = m.da[n]
+        dk = [dot_tn(m.ds[h], q2) for h in range(2)]
+        m.dqkv[3 + n] = (jnp.where(lanes_all, dk[0], dk[1]) * factor).astype(BF16)
+        dv = [dot_tn(m.probs[n, h], d2) for h in range(2)]
+        m.dqkv[6 + n] = jnp.where(lanes_all, dv[0], dv[1]).astype(BF16)
+
+    def side(part, rws):
+        return jnp.concatenate([m.dqkv[3 * part + n, rws, :] for n in range(3)], axis=-1)
+
+    def partial(core):
+        def body(i, _):
+            rws = pl.ds(pl.multiple_of((2 * i + core) * 64, 64), 64)
+            w = dot_nt(side(0, rws), m.wj[0])
+            for part in range(1, 3):
+                w = w + dot_nt(side(part, rws), m.wj[part])
+            m.mp[core, i] = w
+            return 0
+
+        lax.fori_loop(0, chips, body, 0)
+
+    partial(1 - c)
+    start(send_to(m.mp.at[1 - c], m.mp_in, m.pair_sem, 4, b, sibling))
+    partial(c)
+    send_to(m.mp.at[c], m.mp_in, m.pair_sem, 4, b, sibling).wait_recv()
+    for d in range(chips):
+        i = chip(d)
+        low = (m.mp[c, i] + m.mp_in[i]).astype(BF16).reshape(rows // 2, 16, width)
+        if d:
+            m.mo[i] = low
+            start(send_to(m.mo.at[i], m.mr.at[z], m.mr_sem, d, b, 2 * i + c))
+        else:
+            m.mr[z] = low
+
+    for part in range(3):
+        v = m.mg[...].reshape(total, width)
+        w = dot_tn(v, side(part, slice(None)))
+        m.jo[part] = w.astype(BF16).reshape(m.jo.shape[1:])
+        c_one(4 + part).start()
+
+    c_half(2)
+    c_half(3)
+    r_sum()
+
+    for e in range(1, 4):
+        i = lax.rem(b - e + 4, 4)
+        send_to(m.late.at[i, s], m.late.at[i, s], m.late_sem, e, i, s).wait_recv()
+    for d in range(1, chips):
+        start(send_to(m.late.at[:, s], m.late.at[:, s], m.late_sem2, d, b, 2 * chip(d) + c))
+    sums = m.piece[s].astype(F32)
+    for d in range(1, strips):
+        send_to(m.piece.at[0], m.piece_in.at[d], m.piece_sem, d, b, s).wait_recv()
+        sums = sums + m.piece_in[d].astype(F32)
+    m.small[b] = sums.astype(BF16)
+    for e in range(1, 4):
+        start(send_to(m.small.at[b], m.small.at[b], m.small_sem, e, lax.rem(b + e, 4), s))
+
+    for d in range(1, chips):
+        i = chip(chips - d)
+        send_to(m.mo.at[i], m.mr.at[i], m.mr_sem, d, b, 2 * i + c).wait_recv()
+    for r in (0, rows - 1):
+        for p in range(2):
+            m.md[r + 1, p] = m.mr[(r % 2) * 2 + p, r // 2]
+    start_edges(m.md, m.md_sem)
+    for r in range(1, rows - 1):
+        for p in range(2):
+            m.md[r + 1, p] = m.mr[(r % 2) * 2 + p, r // 2]
+
+    m.acc1[...] = jnp.zeros_like(m.acc1)
+
+    def mixer_rows(low, high):
+        for k in range(width // 128):
+            lanes = pl.ds(k * 128, 128)
+            weights = [m.mk[t : t + 1, k * 128 : k * 128 + 128] for t in range(9)]
+
+            def line(r, p):
+                return m.md[r, p, :, lanes]
+
+            def step(r, carry):
+                new = window(line, r + 2)
+                three = (carry[0], carry[1], new)
+                out = conv(three, weights, True)
+                for p in range(2):
+                    m.fg[2 * r + p, :, lanes] = out[p]
+                centre = [m.fp[r + 1, p, :, lanes].astype(F32) for p in range(2)]
+                return carry[1], new, tuple(taps(three, centre, carry[2]))
+
+            begin = tuple(m.acc1[t, :, lanes] for t in range(9))
+            _, _, sums = lax.fori_loop(
+                low, high, step, (window(line, low), window(line, low + 1), begin)
+            )
+            for t in range(9):
+                m.acc1[t, :, lanes] = sums[t]
+
+    m.acc[1] = jnp.zeros_like(m.acc[1])
+    m.acc[2] = jnp.zeros_like(m.acc[2])
+
+    def token_row(r, _):
+        for p in range(2):
+            rp = 2 * r + p
+            grad = m.fg[rp]
+            n, inv = ln_parts(m.xd[r, p].astype(F32))
+            m.acc[1] += grad
+            m.acc[2] += grad * n
+            interleave(m.rowf, r, p, m.rg[rp] + ln_back(grad * scale1, n, inv))
+        m.tgo[r] = joined(m.rowf, r)
+        return 0
+
+    mixer_rows(1, rows - 1)
+    lax.fori_loop(1, rows - 1, token_row, 0)
+    top_edge(m.md, m.md_sem)
+    mixer_rows(0, 1)
+    token_row(0, 0)
+    bottom_edge(m.md, m.md_sem)
+    mixer_rows(rows - 1, rows)
+    token_row(rows - 1, 0)
+    tg_copy = pltpu.make_async_copy(m.tgo, m.tg_hbm, m.load_sem.at[14])
+    tg_copy.start()
+
+    pack = []
+    third = width // 3
+    for v in (m.acc[1], m.acc[2]):
+        pair = halves(v)
+        for h in range(2):
+            pack += [pair[h : h + 1, k * third : k * third + third] for k in range(3)]
+    pack.append(jnp.zeros((4, third), F32))
+    m.early[b, s] = jnp.concatenate(pack, axis=0).astype(BF16)
+    for e in range(1, 4):
+        start(send_to(m.early.at[b, s], m.early.at[b, s], m.early_sem, e, lax.rem(b + e, 4), s))
+    mixer_sums = [jnp.sum(m.acc1[t], axis=0, keepdims=True) for t in range(9)]
+    mixer_sums = jnp.concatenate(mixer_sums + [jnp.zeros((7, width), F32)], axis=0)
+    pad_lanes = jnp.zeros((16, 128 - own), F32)
+    for t in range(strips):
+        m.mpiece[t] = jnp.concatenate(
+            [mixer_sums[:, t * own : t * own + own], pad_lanes], axis=1
+        ).astype(BF16)
+    for d in range(1, strips):
+        t = lax.rem(s + d, strips)
+        start(send_to(m.mpiece.at[t], m.mpiece_in.at[d], m.mpiece_sem, d, b, t))
+
+    c_quarter(0)
+    for j in range(4, 8):
+        c_half(j)
+    for d in range(chips):
+        i = 2 * chip(chips - d) + c
+        if d:
+            send_to(m.late.at[:, i], m.late.at[:, i], m.late_sem2, d, b, i).wait_recv()
+        start(send_to(m.late.at[:, i], m.late.at[:, i], m.late_sem3, d, b, sibling))
+    for e in range(1, 4):
+        i = lax.rem(b - e + 4, 4)
+        send_to(m.early.at[i, s], m.early.at[i, s], m.early_sem, e, i, s).wait_recv()
+    for d in range(1, chips):
+        start(send_to(m.early.at[:, s], m.early.at[:, s], m.early_sem2, d, b, 2 * chip(d) + c))
+    sums = m.mpiece[s].astype(F32)
+    for d in range(1, strips):
+        send_to(m.mpiece.at[0], m.mpiece_in.at[d], m.mpiece_sem, d, b, s).wait_recv()
+        sums = sums + m.mpiece_in[d].astype(F32)
+    m.msmall[b] = sums.astype(BF16)
+    for e in range(1, 4):
+        start(send_to(m.msmall.at[b], m.msmall.at[b], m.msmall_sem, e, lax.rem(b + e, 4), s))
+    c_sum(0)
+    c_quarter(1)
+    for d in range(chips):
+        i = 2 * chip(chips - d) + c
+        if d:
+            send_to(m.early.at[:, i], m.early.at[:, i], m.early_sem2, d, b, i).wait_recv()
+        start(send_to(m.early.at[:, i], m.early.at[:, i], m.early_sem3, d, b, sibling))
+    c_sum(1)
+
+    finals = []
+
+    def store(src, dst, index):
+        cp = pltpu.make_async_copy(src, dst, m.load_sem.at[index])
+        cp.start()
+        finals.append(cp)
+
+    for e in range(1, 4):
+        i = lax.rem(b - e + 4, 4)
+        send_to(m.cond_all.at[i], m.cond_all.at[i], m.cond_sem, e, i, s).wait_recv()
+        send_to(m.small.at[i], m.small.at[i], m.small_sem, e, i, s).wait_recv()
+        send_to(m.msmall.at[i], m.msmall.at[i], m.msmall_sem, e, i, s).wait_recv()
+        send_to(m.r_all.at[i], m.r_all.at[i], m.r4_sem, e, i, s).wait_recv()
+    store(m.r_all, m.r_hbm, 15)
+    store(m.cond_all, m.cond_hbm, 16)
+    store(m.small, m.small_hbm, 17)
+    store(m.msmall, m.msmall_hbm, 18)
+    for d in range(chips):
+        i = 2 * chip(chips - d) + 1 - c
+        send_to(m.late.at[:, i], m.late.at[:, i], m.late_sem3, d, b, sibling).wait_recv()
+        send_to(m.early.at[:, i], m.early.at[:, i], m.early_sem3, d, b, sibling).wait_recv()
+    store(m.late, m.late_hbm, 19)
+    store(m.early, m.early_hbm, 20)
+    for g in range(2):
+        for xs in range(2):
+            for cs in range(2):
+                source = 2 * c + xs
+                e = lax.rem(b - source + 4, 4)
+                local = jnp.logical_and(source == b, cs == c)
+
+                @pl.when(jnp.logical_not(local))
+                def _():
+                    pltpu.make_async_remote_copy(
+                        src_ref=m.c_out.at[g],
+                        dst_ref=m.c_all.at[g, xs, cs],
+                        send_sem=m.c4_sem[0].at[g, e],
+                        recv_sem=m.c4_sem[1].at[g, e, cs],
+                        device_id=(source, 2 * z + cs),
+                        device_id_type=MESH,
+                    ).wait_recv()
+
+    store(m.c_all, m.c_hbm, 21)
+    for cp in sent:
+        cp.wait_send()
+    edges_sent(m.fp, m.fp_sem)
+    edges_sent(m.md, m.md_sem)
+
+    def drain(n, _):
+        halo_sent(m.ex, m.ex_sem, n)
+        halo_sent(m.cg, m.cg_sem, n)
+        r_one(n).wait_send()
+        r_two(n).wait_send()
+        return 0
+
+    lax.fori_loop(0, chips, drain, 0)
+    for j in range(8):
+        c_one(j).wait_send()
+        c_two(j).wait_send()
+    for d in range(1, chips):
+        r_three(d).wait_send()
+        r_four(d).wait_send()
+        for g in range(2):
+            c_three(g, d).wait_send()
+            c_four(g, d).wait_send()
+
+    @pl.when(c != y)
+    def _():
+        for g in range(2):
+            c_four(g, 0).wait_send()
+
+    out_copy.wait()
+    tg_copy.wait()
+    for cp in finals:
+        cp.wait()
+
+
+def block(tokens, mod, mixer, owner, cond, ob, eb, hk, rb, wj, wo, we, wr, cot, strips):
+    rows, cols, width = tokens.shape
+    chips = strips // 2
+    half = width // 2
+    total = strips * 64
+    blocks = 2 * rows
+    chip_rows = 2 * rows
+    part = width // chips // 4
+    third = width // 3
+    shape = jax.ShapeDtypeStruct
+    vm = pltpu.VMEM
+
+    def dma(*size):
+        return pltpu.SemaphoreType.DMA(size)
+
+    ins = dict(
+        tok=tokens, mod=mod, mk=mixer, owner=owner, cond=cond, ob=ob, eb=eb, hk=hk, rb=rb,
+        wj_hbm=wj, wo_hbm=wo, we_hbm=we, wr_hbm=wr, cot_hbm=cot,
+    )
+    outs = dict(
+        out_hbm=shape((rows, cols, width), BF16),
+        tg_hbm=shape((rows, cols, width), F32),
+        r_hbm=shape((4, width // 4, half), BF16),
+        c_hbm=shape((2, 2, 2, 4, part, half), BF16),
+        cond_hbm=shape((4,) + cond.shape, F32),
+        small_hbm=shape((4, 16, half), BF16),
+        msmall_hbm=shape((4, 16, 128), BF16),
+        late_hbm=shape((4, strips, 16, half), BF16),
+        early_hbm=shape((4, strips, 16, third), BF16),
+    )
+    scratch = dict(
+        wj=vm((3, width, half), BF16),
+        wo=vm((width, width), BF16),
+        we=vm((chips, width, half), BF16),
+        wr=vm((chips, half, width), BF16),
+        cot=vm((rows, cols, width), BF16),
+        cond_all=vm((4,) + cond.shape, F32),
+        rowf=vm((rows, width // 128, cols, 128), F32),
+        xd=vm((rows, 2, 16, width), BF16),
+        fp=vm((rows + 2, 2, 16, width), BF16),
+        ms=vm((chips, rows // 2, 16, width), BF16),
+        mg=vm((strips, rows // 2, 16, width), BF16),
+        qkv=vm((9, total, 128), BF16),
+        probs=vm((3, 2, total, total), BF16),
+        ag=vm((6, total, 128), BF16),
+        ai=vm((6, chips, 64, 128), BF16),
+        acc=vm((6, 16, width), F32),
+        acc1=vm((9, 8, width), F32),
+        ctd=vm((blocks, 16, width), BF16),
+        tg=vm((2, blocks, 16, width), BF16),
+        tg_t=vm((width, total), BF16),
+        sc=vm((2, blocks, 16, width), BF16),
+        sc_t=vm((width, total), BF16),
+        b1=vm((blocks, 16, width), F32),
+        res=vm((blocks, 16, width), F32),
+        ex=vm((chips, chip_rows + 2, 2, 16, half), BF16),
+        cg=vm((chips, chip_rows + 2, 2, 16, half), BF16),
+        agr=vm((2 * blocks, 16, half), F32),
+        act=vm((2 * blocks, 16, half), BF16),
+        eg=vm((2 * blocks, 16, half), BF16),
+        b2=vm((2, blocks, 16, width), F32),
+        b2_in=vm((blocks, 16, width), F32),
+        sg=vm((2, blocks, 16, width), F32),
+        sg_in=vm((blocks, 16, width), F32),
+        hkg=vm((chips, 16, half), F32),
+        rg=vm((blocks, 16, width), F32),
+        og=vm((chips, rows // 2, 16, width), BF16),
+        out=vm((rows, cols, width), BF16),
+        gg=vm((strips, rows // 2, 16, width), BF16),
+        da=vm((3, total, 128), BF16),
+        ds=vm((2, total, total), BF16),
+        dqkv=vm((9, total, 128), BF16),
+        mp=vm((2, chips, 64, width), F32),
+        mp_in=vm((chips, 64, width), F32),
+        mo=vm((chips, rows // 2, 16, width), BF16),
+        mr=vm((chips, rows // 2, 16, width), BF16),
+        md=vm((rows + 2, 2, 16, width), BF16),
+        fg=vm((blocks, 16, width), F32),
+        tgo=vm((rows, cols, width), F32),
+        rw=vm((chips, 2, 2, width // 4, half), BF16),
+        r1=vm((chips, 2, width // 4, half), BF16),
+        r2=vm((chips, width // 4, half), BF16),
+        r3=vm((chips, width // 4, half), BF16),
+        r_all=vm((4, width // 4, half), BF16),
+        ew=vm((4, chips, 2, 2, part, half), BF16),
+        jo=vm((4, chips, 2, 2, part, half), BF16),
+        c1=vm((8, chips, 2, part, half), BF16),
+        c2=vm((8, chips, part, half), BF16),
+        c3=vm((2, chips, 4, part, half), BF16),
+        c_out=vm((2, 4, part, half), BF16),
+        c_all=vm((2, 2, 2, 4, part, half), BF16),
+        late=vm((4, strips, 16, half), BF16),
+        early=vm((4, strips, 16, third), BF16),
+        piece=vm((strips, 16, half), BF16),
+        piece_in=vm((strips, 16, half), BF16),
+        small=vm((4, 16, half), BF16),
+        mpiece=vm((strips, 16, 128), BF16),
+        mpiece_in=vm((strips, 16, 128), BF16),
+        msmall=vm((4, 16, 128), BF16),
+        load_sem=dma(22),
+    )
+    pairs = dict(
+        cond_sem=(4,), fp_sem=(2,), md_sem=(2,), mg_sem=(chips,), mg_sem2=(chips,),
+        gg_sem=(chips,), gg_sem2=(chips,), ai_sem=(3, strips), ag_sem=(3,), pair_sem=(5,),
+        ex_sem=(2, chips), cg_sem=(2, chips), mr_sem=(chips,),
+        r1_sem=(chips,), r2_sem=(chips,), r3_sem=(chips,), r4_sem=(4,),
+        c1_sem=(8,), c2_sem=(8,), c3_sem=(2, chips),
+        late_sem=(4,), late_sem2=(chips,), late_sem3=(chips,),
+        early_sem=(4,), early_sem2=(chips,), early_sem3=(chips,),
+        piece_sem=(strips,), small_sem=(4,), mpiece_sem=(strips,), msmall_sem=(4,),
+    )
+    names = list(ins) + list(outs) + list(scratch)
+    shapes = list(scratch.values())
+    for size in list(pairs.values()):
+        shapes += [dma(*size), dma(*size)]
+    shapes += [dma(2, 4), dma(2, 4, 2)]
+    plain = len(names)
+
+    def kernel(*refs):
+        named = list(refs[:plain])
+        sems = refs[plain:]
+        both = [(sems[2 * i], sems[2 * i + 1]) for i in range(len(sems) // 2)]
+        block_kernel(names + list(pairs) + ["c4_sem"], *named, *both)
+
+    return pl.pallas_call(
+        kernel,
+        name="block",
+        out_shape=tuple(outs.values()),
+        in_specs=[WHOLE] * 3 + [SCALARS] + [WHOLE] * 5 + [LEFT] * 5,
+        out_specs=(LEFT,) * len(outs),
+        scratch_shapes=shapes,
+        compiler_params=pltpu.CompilerParams(
+            collective_id=0, has_side_effects=True, vmem_limit_bytes=VMEM_BYTES
+        ),
+    )(*ins.values())
+
+
+def final_kernel(
+    out_in, tg_in, r_ref, c_ref, cond_ref, small_ref, msmall_ref, late_ref, early_ref, aw_hbm,
+    out_ref, tg_ref, tab_ref, ad_ref, ab_ref, mix_ref, joint_ref, output_ref, ob_ref,
+    expand_ref, eb_ref, hidden_ref, reduce_ref, rb_ref,
+    aw, out_v, tg_v, sem,
+):
+    s = lax.axis_index("strip")
+    strips = lax.axis_size("strip")
+    width = cond_ref.shape[2] - 256
+    own = width // strips
+    half = width // 2
+    third = width // 3
+    copies = [
+        pltpu.make_async_copy(out_in, out_v, sem.at[0]),
+        pltpu.make_async_copy(tg_in, tg_v, sem.at[1]),
+        pltpu.make_async_copy(aw_hbm.at[pl.ds(pl.multiple_of(s * own, 16), own)], aw, sem.at[2]),
+    ]
+    for cp in copies:
+        cp.start()
+
+    stores = [
+        pltpu.make_async_copy(out_v, out_ref, sem.at[3]),
+        pltpu.make_async_copy(tg_v, tg_ref, sem.at[4]),
+    ]
+
+    small = small_ref[0].astype(F32)
+    mixer = msmall_ref[0].astype(F32)
+    for i in range(1, 4):
+        small = small + small_ref[i].astype(F32)
+        mixer = mixer + msmall_ref[i].astype(F32)
+    hidden_ref[...] = small[0:9]
+    eb_ref[...] = small[9:10]
+    ob_ref[...] = small[10:11, 0:own]
+    rb_ref[...] = small[11:12, 0:own]
+    mix_ref[...] = mixer[0:9, 0:own]
+
+    for i in range(2):
+        copies[i].wait()
+        stores[i].start()
+
+    n = r_ref.shape[1]
+    for q in range(4):
+        reduce_ref[:, q * n : q * n + n] = r_ref[q].astype(F32).T
+    part = c_ref.shape[4]
+    for xs in range(2):
+        rows = slice(xs * part, xs * part + part)
+        for cs in range(2):
+            for k in range(4):
+                at = (2 * k + cs) * half
+                expand_ref[rows, at : at + half] = c_ref[0, xs, cs, k].astype(F32)
+                if k < 3:
+                    joint_ref[rows, at : at + half] = c_ref[1, xs, cs, k].astype(F32)
+            output_ref[rows, cs * half : cs * half + half] = c_ref[1, xs, cs, 3].astype(F32)
+
+    slots = 32
+    condition = cond_ref[...].reshape(slots, width + 256)
+    labels = condition[:, width : width + 1]
+    slot_late = jnp.concatenate([cond_ref[i, 0:1, width + 128 :] for i in range(4)], axis=1)
+    slot_early = jnp.concatenate([cond_ref[i, 1:2, width + 128 :] for i in range(4)], axis=1)
+    condition = condition[:, 0:width]
+    pick = lax.broadcasted_iota(jnp.int32, (width, own), 0) == (
+        lax.broadcasted_iota(jnp.int32, (width, own), 1) + s * own
+    )
+    pick = jnp.where(pick, 1.0, 0.0)
+    condition = jnp.dot(
+        condition, pick, precision=lax.Precision.HIGHEST, preferred_element_type=F32
+    )
+    sigmoid = 1.0 / (1.0 + jnp.exp(-condition))
+    silu = (condition * sigmoid).astype(BF16)
+    slope = sigmoid * (1.0 + condition * (1.0 - sigmoid))
+
+    count = 4 * strips * 16
+    row = lax.rem(lax.broadcasted_iota(jnp.int32, (slots, count), 1), 16)
+    index = lax.broadcasted_iota(jnp.int32, (slots, count), 0)
+    hit_late = index == slot_late.astype(jnp.int32)
+    hit_early = index == slot_early.astype(jnp.int32)
+    late = late_ref[...].reshape(count, half)
+    early = early_ref[...].reshape(count, third)
+    copies[2].wait()
+    silu_grad = jnp.zeros((slots, own), F32)
+    pieces = []
+    for i in range(2):
+        for k in range(3):
+            mine = jnp.logical_or(row == 6 * i + k, row == 6 * i + 3 + k)
+            pieces.append((early, jnp.logical_and(hit_early, mine), i * width + k * third, third))
+    for i in range(4):
+        for k in range(2):
+            mine = jnp.logical_or(row == 4 * i + k, row == 4 * i + 2 + k)
+            pieces.append((late, jnp.logical_and(hit_late, mine), (2 + i) * width + k * half, half))
+    for source, mine, at, size in pieces:
+        chosen = jnp.where(mine, 1.0, 0.0).astype(BF16)
+        grad = dot(chosen, source)
+        ab_ref[:, at : at + size] = jnp.sum(grad, axis=0, keepdims=True)
+        low = grad.astype(BF16)
+        ad_ref[:, at : at + size] = dot_tn(silu, low)
+        silu_grad = silu_grad + dot_nt(low, aw[:, at : at + size])
+    classes = tab_ref.shape[1]
+    onehot = lax.broadcasted_iota(jnp.int32, (slots, classes), 1) == labels.astype(jnp.int32)
+    tab_ref[...] = lax.dot_general(
+        silu_grad * slope,
+        jnp.where(onehot, 1.0, 0.0),
+        TN,
+        precision=lax.Precision.HIGHEST,
+        preferred_element_type=F32,
+    )
+    for cp in stores:
+        cp.wait()
+
+
+def final(parts, aw, classes, strips):
+    out, tg, r, c, cond, small, msmall, late, early = parts
+    width = out.shape[-1]
+    own = width // strips
+    half = width // 2
+    shape = jax.ShapeDtypeStruct
+    return pl.pallas_call(
+        final_kernel,
+        name="final",
+        out_shape=(
+            shape(out.shape, BF16),
+            shape(tg.shape, F32),
+            shape((own, classes), F32),
+            shape((own, 6 * width), F32),
+            shape((1, 6 * width), F32),
+            shape((9, own), F32),
+            shape((own, 3 * width), F32),
+            shape((own, width), F32),
+            shape((1, own), F32),
+            shape((own, 4 * width), F32),
+            shape((1, half), F32),
+            shape((9, half), F32),
+            shape((half, width), F32),
+            shape((1, own), F32),
+        ),
+        in_specs=[LEFT] * 2 + [WHOLE] * 7 + [LEFT],
+        out_specs=(LEFT,) * 2 + (WHOLE,) * 12,
+        scratch_shapes=[
+            pltpu.VMEM((own, 6 * width), BF16),
+            pltpu.VMEM(out.shape, BF16),
+            pltpu.VMEM(tg.shape, F32),
+            pltpu.SemaphoreType.DMA((5,)),
+        ],
+        compiler_params=pltpu.CompilerParams(vmem_limit_bytes=VMEM_BYTES),
+    )(out, tg, r, c, cond, small, msmall, late, early, aw)
+
+
+def timestep_features(time_steps, model_width):
+    half_width = model_width // 2
+    frequencies = jnp.exp(
+        -math.log(10000.0) * jnp.arange(half_width, dtype=F32) / half_width
+    )
+    angles = time_steps.astype(F32)[..., None] * frequencies
+    return jnp.concatenate([jnp.cos(angles), jnp.sin(angles)], axis=-1)
+
+
+def local_grouped(
+    tokens, tile_owner, time_steps, class_labels, class_embedding_matrix, adaptive_weight,
+    adaptive_bias, mixer_kernel, joint_weight, output_weight, output_bias, expand_weight,
+    expand_bias, hidden_kernel, reduce_weight, reduce_bias, output_cotangent,
+):
+    _, rows, cols, width = tokens.shape
+    strips = lax.axis_size("strip")
+    s = lax.axis_index("strip")
+    b = lax.axis_index("batch")
+    classes = class_embedding_matrix.shape[1]
+    latents = time_steps.shape[1]
+    own = width // strips
+    piece = expand_weight.shape[1] // strips
+    owner = tile_owner[0].reshape(-1)
+
+    onehot = (class_labels[0][:, None] == jnp.arange(classes, dtype=jnp.int32)).astype(BF16)
+    condition = timestep_features(time_steps[0], width) + jnp.einsum(
+        "bn,dn->bd", onehot, class_embedding_matrix, preferred_element_type=F32
+    )
+    silu_cond = jax.nn.silu(condition).astype(BF16)
+    modulation = jnp.dot(silu_cond, adaptive_weight, preferred_element_type=F32)
+    modulation = modulation + adaptive_bias.astype(F32)
+    pair = lax.dynamic_slice_in_dim(owner, 2 * (s * 4 // strips), 2)
+    mod = jnp.dot(
+        (pair[:, None] == jnp.arange(latents, dtype=jnp.int32)).astype(F32),
+        modulation,
+        precision=lax.Precision.HIGHEST,
+    )
+    labels = jnp.broadcast_to(class_labels[0].astype(F32)[:, None], (latents, 128))
+    slot_late = jnp.broadcast_to(
+        (tile_owner[0] + b * latents).astype(F32)[:, None, None, :, None],
+        (4, strips // 4, 4, 2, 2),
+    ).reshape(1, -1)
+    slot_early = jnp.broadcast_to(
+        (tile_owner[0] + b * latents).astype(F32)[:, None, :, None], (4, 2, 2, 3)
+    ).reshape(4, 1, 12)
+    slot_early = jnp.broadcast_to(
+        jnp.pad(slot_early, ((0, 0), (0, 0), (0, 4))), (4, strips // 4, 16)
+    ).reshape(1, -1)
+    slots = jnp.concatenate([slot_late] + [slot_early] * (latents - 1), axis=0)
+    cond = jnp.concatenate([condition, labels, slots], axis=1)
+    mixer = mixer_kernel.T.astype(F32)
+    hidden = hidden_kernel.T.astype(F32).reshape(9, strips, piece).transpose(1, 0, 2)
+    parts = block(
+        tokens[0], mod, mixer, owner, cond, output_bias.astype(F32)[None],
+        expand_bias.astype(F32).reshape(strips, 1, piece), hidden,
+        reduce_bias.astype(F32)[None], joint_weight, output_weight, expand_weight,
+        reduce_weight, output_cotangent[0], strips,
+    )
+    (
+        out, tg, table, adaptive, bias, mix, joint, output, ob, expand, eb, hid, reduce, rb,
+    ) = final(parts, adaptive_weight, classes, strips)
+    bias = lax.dynamic_slice_in_dim(bias.reshape(-1), s * 6 * own, 6 * own)
+    return (
+        out[None], tg[None], table, adaptive, bias, mix.T, joint, output, ob.reshape(-1),
+        expand, eb.reshape(-1), hid.T, reduce, rb.reshape(-1),
+    )
+
+
 EXACT_PRECISION = lax.Precision.HIGHEST
 
 
@@ -68,15 +1446,6 @@
         ]
         columns.append(jnp.sum(window * gradient, axis=(0, 1, 2)))
     return jnp.stack(columns, axis=1)
-
-
-def timestep_features(time_steps, model_width):
-    half_width = model_width // 2
-    frequencies = jnp.exp(
-        -math.log(10000.0) * jnp.arange(half_width, dtype=jnp.float32) / half_width
-    )
-    angles = time_steps.astype(jnp.float32)[..., None] * frequencies
-    return jnp.concatenate([jnp.cos(angles), jnp.sin(angles)], axis=-1)
 
 
 def group_owner(owner):
@@ -446,8 +1815,9 @@
 
 
 def solution(mesh):
+    grouped = (mesh.shape["batch"], mesh.shape["strip"]) == (4, 8)
     return jax.shard_map(
-        local,
+        local_grouped if grouped else local,
         mesh=mesh,
         in_specs=(
             P("batch", "strip", None, None),

time: 880 us -> 217 us (0.25)
  waiting for transfers between devices: 367 us -> 0 us
  Pallas kernels: 0 us -> 196 us
  local copies, waits for them, and re-layouts: 180 us -> 6.25 us
  matrix products: 133 us -> 5.95 us
  blocking collectives: 99.5 us -> 0 us
  other arithmetic: 56 us -> 6.78 us
  starting transfers between devices: 17.7 us -> 0 us
  between operations: 17.7 us -> 0.75 us
    reduce_scatter x6 -> x0, waiting for transfers between devices: 226 us -> none  [the longest x1 78.1 us: local(): lax.psum_scatter(adaptive_grad.astype(jnp.bfloat16), 'strip', scatter_dim...]
    pallas_call x0 -> x2, Pallas kernels: none -> 196 us  [the longest x1 187 us: block(): pl.pallas_call(kernel, name='block', out_shape=tuple(outs.values()), in_s...]
    dot_general x26 -> x3, matrix products: 133 us -> 5.95 us  [the longest x1 4.05 us: local_grouped(): modulation = jnp.dot(silu_cond, adaptive_weight, preferred_element_type=F32)]
    unnamed x15 -> x0, waiting for transfers between devices: 60.8 us -> none
    all_gather x2 -> x0, blocking collectives: 54.3 us -> none  [the longest x1 36.2 us: local(): lax.all_gather(log_total[..., 0], 'strip', axis=4, tiled=True)]
    all_gather x4 -> x0, waiting for transfers between devices: 45.6 us -> none  [the longest x1 25.3 us: local(): lax.all_gather(keys_local, 'strip', axis=1, tiled=True)]
    all_gather x4 -> x0, local copies, waits for them, and re-layouts: 35.2 us -> none  [the longest x1 15.4 us: local(): lax.all_gather(query_groups, 'strip', axis=4, tiled=True)]
    reshape x9 -> x3, local copies, waits for them, and re-layouts: 35.2 us -> 0.32 us  [the longest x1 0.15 us: local_grouped(): slot_late = jnp.broadcast_to((tile_owner[0] + b * latents).astype(F32)[:,...]
  transfers between devices with their start and end apart: 21 -> 0, of which waited for: 12 -> 0; matrix products, arithmetic and copies ran while one was open for 28% -> 0% of each run, Pallas kernels for 0% -> 0%
where the time goes in v2:
time: 217 us; the launch traced here: 216 us
  Pallas kernels  196 us (90%)
  other arithmetic  6.78 us (3%)
  local copies, waits for them, and re-layouts  6.25 us (3%)
  matrix products  5.95 us (3%)
    pallas_call x1, Pallas kernels, block(): pl.pallas_call(kernel, name='block', out_shape=tuple(outs.values()), in_s...  187 us
    pallas_call x1, Pallas kernels, final(): pl.pallas_call(final_kernel, name='final', out_shape=(shape(out.shape, BF...  9.3 us

profile of v2, /device:TPU:0, one launch (start us, length us, event | category | flops | bytes accessed | tf_op | source)
XLA Modules:
  0.0 216.1 jit_solution(7199610992520966028)
XLA Ops:
  0.7 0.8 convert_bitcast_fusion.2
  1.5 0.7 convert_bitcast_fusion.1
  2.1 0.7 bitcast_convert_fusion
  2.8 0.1 copy.35
  2.9 0.8 copy.34
  3.7 0.1 reshape_squeeze.3.refs_3_
  3.8 1.3 reshape.100.refs_5_
  5.1 1.3 reshape.103.refs_8_
  6.5 0.1 reshape.92
  6.6 0.1 reshape.93
  6.7 1.3 reshape.101
  8.0 0.7 convert_element_type.57
  8.7 0.1 multiply_cosine_fusion
  8.8 1.0 convolution_add_fusion.1
  9.9 0.1 reshape.91
  10.1 0.6 pad_maximum_fusion.refs_4_
  10.7 0.6 convert_bitcast_fusion.refs_2_
  11.3 4.1 %convolution_add_fusion = f32[8,4608]{1,0:T(8,128)S(1)} fusion(bf16[768,4608]{1,0:T(8,128)(2,1)} %aw_hbm.1, f32[4608]{0:T(1024)S(1)} %convert_element_type.57, f32[8,768]{1,0:T(8,128)S(1)} %convolution_add_fusion.1), kind=kOutput, calls=%fused_computation | convolution fusion | flops 56690688 | bytes 7268352 | tf_op jit(solution)/shard_map/dot_general | solution.py:1352
  15.4 0.9 fusion.2.refs_1_
  16.4 0.7 copy.40
  17.1 187.1 %block.1 = (bf16[8,32,768]{2,1,0:T(8,128)(2,1)}, f32[8,32,768]{2,1,0:T(8,128)}, bf16[4,192,384]{2,1,0:T(8,128)(2,1)}, bf16[2,2,2,4,48,384]{5,4,3,2,1,0:T(8,128)(...) custom-call(bf16[8,32,768]{2,1,0:T(8,128)(2,1)} %bitcast.32, ...), custom_call_target="tpu_custom_call" | custom-call | tf_op jit(solution)/shard_map/block/pallas_call | solution.py:1164
  204.2 9.3 %final.1 = (bf16[8,32,768]{2,1,0:T(8,128)(2,1)}, f32[8,32,768]{2,1,0:T(8,128)}, f32[96,1000]{1,0:T(8,128)}, f32[96,4608]{1,0:T(8,128)}, f32[1,4608]{1,0:T(1,128)...) custom-call(bf16[8,32,768]{2,1,0:T(8,128)(2,1)} %get-tuple-element.3, ...), custom_call_target="tpu_custom_call" | custom-call | tf_op jit(solution)/shard_map/final/pallas_call | solution.py:1292
  213.5 1.3 reduce.1
  214.7 1.3 dynamic-slice_reduce_fusion
  (19 shorter events, 0.4 us)
Async XLA Ops:
  0.6 8.2 %copy-start = (bf16[768,1000]{0,1:T(8,128)(2,1)S(1)}, bf16[768,1000]{0,1:T(8,128)(2,1)}, u32[]{:S(2)}) copy-start(bf16[768,1000]{0,1:T(8,128)(2,1)} %param.21) | copy-start | bytes 4608004
  0.7 10.1 %copy-start.2 = (bf16[768,9]{0,1:T(8,128)(2,1)S(1)}, bf16[768,9]{0,1:T(8,128)(2,1)}, u32[]{:S(2)}) copy-start(bf16[768,9]{0,1:T(8,128)(2,1)} %param.24) | copy-start | bytes 41476
  3.7 11.7 %copy-start.3 = (s32[8]{0:T(128)}, s32[8]{0:T(128)S(1)}, u32[]{:S(2)}) copy-start(s32[8]{0:T(128)S(1)} %reshape_squeeze.3.refs_3_) | copy-start | bytes 100
  11.3 5.0 %copy-start.1 = (bf16[3072,9]{0,1:T(8,128)(2,1)S(1)}, bf16[3072,9]{0,1:T(8,128)(2,1)}, u32[]{:S(2)}) copy-start(bf16[3072,9]{0,1:T(8,128)(2,1)} %param.30) | copy-start | bytes 165892
